TPU v7x, 32 devices: a whole 2x2x4 slice. The times are simulated.
32 devices in a mesh: seq: 8 (over z, x), ch: 4 (over y, core).
Axes of the slice: x: 2, y: 2, z: 4, core: 2. Of those that a mesh axis runs over, the one named last changes fastest.
Arguments:
- queries_in: bfloat16 [2048, 8192], P('seq', 'ch'), may hold values from -160 to 160
- keys_in: bfloat16 [2048, 8192], P('seq', 'ch'), may hold values from -8 to 8
- values_in: bfloat16 [2048, 8192], P('seq', 'ch'), may hold values from -6 to 6
- gate_branch: bfloat16 [2048, 8192], P('seq', 'ch'), may hold values from -6 to 6
- key_branch: bfloat16 [2048, 8192], P('seq', 'ch'), may hold values from -6 to 6
- mr_filter: bfloat16 [128, 8192], P(None, 'ch'), may hold values from -3 to 3
- out_grad: bfloat16 [2048, 8192], P('seq', 'ch'), may hold values from -40 to 40
- doc_ids: int32 [2048], replicated, may hold values from 0 to 15, never falling along the last dimension, each value on 1 to 1024 neighbouring positions
Outputs:
- query_grad: bfloat16 [2048, 8192], P('seq', 'ch')
- key_grad: bfloat16 [2048, 8192], P('seq', 'ch')
- value_grad: bfloat16 [2048, 8192], P('seq', 'ch')
- gate_grad: bfloat16 [2048, 8192], P('seq', 'ch')
- branch_grad: bfloat16 [2048, 8192], P('seq', 'ch')
- filter_step: float32 [128, 8192], P('seq', 'ch')
Inputs may be any that keep to these rules, and one draw needn't show every extreme that they name: `doc_ids`: document numbers never fall along the sequence; each document has 1 to 1024 tokens and one has exactly 1024.
All inputs are finite; a program needn't handle non-finite values.
Results may differ from a plain program's by a relative error of at most 0.009.
Values may be sent and summed in bfloat16 or wider, within the bound.
A program may use at most 128 MiB of HBM per device.

v0:
```python
import jax
import jax.numpy as jnp
from jax import lax
from jax.sharding import PartitionSpec as P

HD = 128
TAPS = 128
SPAN = 4


def from_behind(array, axis, by):
    size = lax.axis_size(axis)
    pairs = [(i, i + by) for i in range(size) if 0 <= i + by < size]
    return lax.ppermute(array, axis, pairs)


def causal_conv(extended, weights_in):
    channels = extended.shape[1]
    kernel = jnp.flip(weights_in, 0)[:, None, :]
    result = lax.conv_general_dilated(
        extended[None],
        kernel,
        (1,),
        "VALID",
        dimension_numbers=("NWC", "WIO", "NWC"),
        feature_group_count=channels,
        preferred_element_type=jnp.float32,
    )
    return result[0]


def anti_conv(extended, weights_in):
    channels = extended.shape[1]
    kernel = weights_in[:, None, :]
    result = lax.conv_general_dilated(
        extended[None],
        kernel,
        (1,),
        "VALID",
        dimension_numbers=("NWC", "WIO", "NWC"),
        feature_group_count=channels,
        preferred_element_type=jnp.float32,
    )
    return result[0]


def filter_corr(extended, gradient):
    channels = extended.shape[1]
    kernel = gradient[:, None, :]
    result = lax.conv_general_dilated(
        extended[None],
        kernel,
        (1,),
        "VALID",
        dimension_numbers=("NWC", "WIO", "NWC"),
        feature_group_count=channels,
        preferred_element_type=jnp.float32,
    )
    return jnp.flip(result[0], 0)


def per_device(
    queries_in, keys_in, values_in, gate_branch, key_branch, mr_filter, out_grad, doc_ids
):
    shard_len = queries_in.shape[0]
    width = queries_in.shape[1]
    heads_dev = width // HD
    window = (SPAN + 1) * shard_len
    score_scale = HD ** (-0.5)
    position = lax.axis_index("seq")
    earlier = []
    current = (keys_in, values_in)
    for offset in range(SPAN):
        current = from_behind((current[0], current[1]), "seq", 1)
        earlier.append(current)
    key_win = jnp.concatenate(
        [earlier[SPAN - 1 - index][0] for index in range(SPAN)] + [keys_in], 0
    ).reshape(window, heads_dev, HD)
    value_win = jnp.concatenate(
        [earlier[SPAN - 1 - index][1] for index in range(SPAN)] + [values_in], 0
    ).reshape(window, heads_dev, HD)
    doc_front = jnp.concatenate([jnp.full((SPAN * shard_len,), -1, jnp.int32), doc_ids], 0)
    key_doc = lax.dynamic_slice_in_dim(doc_front, position * shard_len, window, 0)
    query_doc = lax.dynamic_slice_in_dim(doc_ids, position * shard_len, shard_len, 0)
    query_pos = position * shard_len + jnp.arange(shard_len, dtype=jnp.int32)
    key_pos = (position - SPAN) * shard_len + jnp.arange(window, dtype=jnp.int32)
    allowed = (query_doc[:, None] == key_doc[None, :]) & (key_pos[None, :] <= query_pos[:, None])
    queries = queries_in.reshape(shard_len, heads_dev, HD)
    scores = (
        jnp.einsum("qhd,khd->hqk", queries, key_win, preferred_element_type=jnp.float32)
        * score_scale
    )
    scores = jnp.where(allowed[None], scores, -jnp.inf)
    row_max = jnp.max(scores, -1)
    log_total = row_max + jnp.log(jnp.sum(jnp.exp(scores - row_max[..., None]), -1))
    weights = jnp.where(allowed[None], jnp.exp(scores - log_total[..., None]), 0.0)
    probs = weights.astype(jnp.bfloat16)
    attn_out = (
        jnp.einsum("hqk,khd->qhd", probs, value_win, preferred_element_type=jnp.float32)
        .astype(jnp.bfloat16)
        .reshape(shard_len, width)
    )
    mixed = (key_branch.astype(jnp.float32) * attn_out.astype(jnp.float32)).astype(jnp.bfloat16)
    mixed_edge = from_behind(mixed[shard_len - (TAPS - 1) :], "seq", 1)
    mixed_ext = jnp.concatenate([mixed_edge, mixed], 0)
    conv_out = causal_conv(mixed_ext, mr_filter)
    gate_grad = (out_grad.astype(jnp.float32) * conv_out).astype(jnp.bfloat16)
    conv_grad = (out_grad.astype(jnp.float32) * gate_branch.astype(jnp.float32)).astype(
        jnp.bfloat16
    )
    grad_edge = from_behind(conv_grad[: TAPS - 1], "seq", -1)
    mixed_grad = anti_conv(jnp.concatenate([conv_grad, grad_edge], 0), mr_filter)
    filter_part = filter_corr(mixed_ext, conv_grad)
    branch_grad = (mixed_grad * attn_out.astype(jnp.float32)).astype(jnp.bfloat16)
    attn_grad = (mixed_grad * key_branch.astype(jnp.float32)).astype(jnp.bfloat16)
    out_grads = attn_grad.reshape(shard_len, heads_dev, HD)
    out_rows = attn_out.reshape(shard_len, heads_dev, HD)
    row_dot = jnp.einsum("qhd,qhd->hq", out_grads, out_rows, preferred_element_type=jnp.float32)
    prob_grad = jnp.einsum("qhd,khd->hqk", out_grads, value_win, preferred_element_type=jnp.float32)
    score_grad = (weights * (prob_grad - row_dot[..., None])).astype(jnp.bfloat16)
    query_grad = (
        (
            jnp.einsum("hqk,khd->qhd", score_grad, key_win, preferred_element_type=jnp.float32)
            * score_scale
        )
        .astype(jnp.bfloat16)
        .reshape(shard_len, width)
    )
    key_terms = (
        jnp.einsum("hqk,qhd->khd", score_grad, queries, preferred_element_type=jnp.float32)
        * score_scale
    ).reshape(window, width)
    value_terms = jnp.einsum(
        "hqk,qhd->khd", probs, out_grads, preferred_element_type=jnp.float32
    ).reshape(window, width)
    key_sum = key_terms[SPAN * shard_len :]
    value_sum = value_terms[SPAN * shard_len :]
    for offset in range(SPAN):
        first_row = (SPAN - 1 - offset) * shard_len
        back_key, back_value = from_behind(
            (
                key_terms[first_row : first_row + shard_len],
                value_terms[first_row : first_row + shard_len],
            ),
            "seq",
            -(offset + 1),
        )
        key_sum = key_sum + back_key
        value_sum = value_sum + back_value
    tap_rows = TAPS // lax.axis_size("seq")
    filter_grad = lax.psum(filter_part, "seq")
    filter_sq = jnp.sum(jnp.square(mr_filter.astype(jnp.float32)))
    norms = lax.psum((filter_sq, jnp.sum(filter_grad * filter_grad)), "ch")
    own_grad = lax.dynamic_slice_in_dim(filter_grad, position * tap_rows, tap_rows, 0)
    trust = jnp.sqrt(norms[0]) / jnp.sqrt(norms[1] + 1e-06)
    filter_step = trust * own_grad
    return (
        query_grad,
        key_sum.astype(jnp.bfloat16),
        value_sum.astype(jnp.bfloat16),
        gate_grad,
        branch_grad,
        filter_step,
    )


def solution(mesh):
    return jax.shard_map(
        per_device,
        mesh=mesh,
        in_specs=(
            P("seq", "ch"),
            P("seq", "ch"),
            P("seq", "ch"),
            P("seq", "ch"),
            P("seq", "ch"),
            P(None, "ch"),
            P("seq", "ch"),
            P(),
        ),
        out_specs=(
            P("seq", "ch"),
            P("seq", "ch"),
            P("seq", "ch"),
            P("seq", "ch"),
            P("seq", "ch"),
            P("seq", "ch"),
        ),
        check_vma=False,
    )
```

profile of v0, /device:TPU:14, one launch (start us, length us, event | category | flops | bytes accessed | tf_op | source)
XLA Modules:
  0.0 910.9 jit_solution(4401209401382365496)
XLA Ops:
  8.9 3.5 collective-permute-start
  14.6 3.5 collective-permute-start.5
  18.1 18.8 %collective-permute-done = bf16[256,2048]{0,1:T(8,128)(2,1)} collective-permute-done((bf16[256,2048]{0,1:T(8,128)(2,1)S(1)}, bf16[256,2048]{0,1:T(8,128)(2,1)}, u32[]{:S(2)}, u32[]{:S(2)}) %collective-permute-start) | collective-permute-done | bytes 1048608 | tf_op jit(solution)/shard_map/ppermute | solution.py:14
  36.9 4.3 collective-permute-start.1
  45.2 8.4 rev.8
  53.7 16.9 %collective-permute-done.5 = bf16[256,2048]{0,1:T(8,128)(2,1)} collective-permute-done((bf16[256,2048]{0,1:T(8,128)(2,1)}, bf16[256,2048]{0,1:T(8,128)(2,1)}, u32[]{:S(2)}, u32[]{:S(2)}) %collective-permute-start.5) | collective-permute-done | bytes 1048608 | tf_op jit(solution)/shard_map/ppermute | solution.py:14
  70.6 2.5 collective-permute-start.6
  73.1 20.0 %collective-permute-done.1 = bf16[256,2048]{0,1:T(8,128)(2,1)} collective-permute-done((bf16[256,2048]{0,1:T(8,128)(2,1)}, bf16[256,2048]{0,1:T(8,128)(2,1)}, u32[]{:S(2)}, u32[]{:S(2)}) %collective-permute-start.1) | collective-permute-done | bytes 1048608 | tf_op jit(solution)/shard_map/ppermute | solution.py:14
  93.1 2.5 collective-permute-start.2
  98.4 37.3 %collective-permute-done.4 = bf16[127,2048]{1,0:T(8,128)(2,1)} collective-permute-done((bf16[127,2048]{1,0:T(8,128)(2,1)S(1)}, bf16[127,2048]{1,0:T(8,128)(2,1)}, u32[]{:S(2)}, u32[]{:S(2)}) %collective-permute-start.4) | collective-permute-done | bytes 520224 | tf_op jit(solution)/shard_map/ppermute | solution.py:14
  136.9 5.5 collective-permute-start.7
  144.4 29.1 %fusion.1 = f32[1,256,2048]{2,0,1:T(1,128)} fusion(bf16[1,383,2048]{2,1,0:T(8,128)(2,1)S(1)} %maximum_bitcast_fusion, bf16[128,1,2048]{2,0,1:T(8,128)(2,1)S(1)} %bitcast.83), kind=kOutput, calls=%fused_computation.7 | convolution fusion | flops 134217728 | bytes 4190208 | tf_op jit(solution)/shard_map/conv_general_dilated | solution.py:35
  173.4 5.1 collective-permute-start.8
  178.6 9.9 %collective-permute-done.3 = bf16[256,2048]{0,1:T(8,128)(2,1)S(1)} collective-permute-done((bf16[256,2048]{0,1:T(8,128)(2,1)S(1)}, bf16[256,2048]{0,1:T(8,128)(2,1)S(1)}, u32[]{:S(2)}, u32[]{:S(2)}) %collective-permute-start.3) | collective-permute-done | bytes 1048608 | tf_op jit(solution)/shard_map/ppermute | solution.py:14
  191.3 18.6 %collective-permute-done.8 = bf16[256,2048]{0,1:T(8,128)(2,1)S(1)} collective-permute-done((bf16[256,2048]{0,1:T(8,128)(2,1)S(1)}, bf16[256,2048]{0,1:T(8,128)(2,1)S(1)}, u32[]{:S(2)}, u32[]{:S(2)}) %collective-permute-start.8) | collective-permute-done | bytes 1048608 | tf_op jit(solution)/shard_map/ppermute | solution.py:14
  218.0 9.0 fusion.22
  226.9 8.7 exponential_reduce_fusion
  235.6 12.3 %convolution_convert_fusion = bf16[16,128,256]{2,1,0:T(8,128)(2,1)S(1)} fusion(bf16[1280,16,128]{0,2,1:T(8,128)(2,1)} %bitcast.6, f32[16,256,1280]{1,2,0:T(8,128)} %get-tuple-element.34, f32[16,256]{1,0:T(8,128)S(1)} %log_add_fusion, pred[256,1280]{0,1:T(8,128)(4,1)S(1)} %compare_and_fusion), kind=kOutput, calls=%fused_computation.30 | convolution fusion | flops 1358430208 | bytes 27607040 | tf_op jit(solution)/shard_map/hqk,khd->qhd/dot_general | solution.py:99
  251.0 5.1 fusion.11
  258.7 3.1 copy.84
  263.6 15.6 %multiply_convert_fusion = bf16[16,256,1280]{1,2,0:T(8,128)(2,1)} fusion(bf16[256,16,128]{0,2,1:T(8,128)(2,1)S(1)} %copy.62, bf16[1280,16,128]{0,2,1:T(8,128)(2,1)} %bitcast.6, f32[16,256,1280]{1,2,0:T(8,128)} %get-tuple-element.34, f32[16,256]{1,0:T(8,128)S(1)} %multiply_reduce_fusion, f32[16,256]{1,0:T(8,128)S(1)} %log_add_fusion, ...), kind=kOutput, calls=%fused_computation.1 | convolution fusion | flops 1368391680 | bytes 38109184 | tf_op jit(solution)/shard_map/qhd,khd->hqk/dot_general | solution.py:119
  279.3 7.1 multiply_convert_fusion.1
  286.3 11.4 %multiply_bitcast_fusion = f32[1280,16,128]{0,2,1:T(8,128)} fusion(bf16[16,256,1280]{1,2,0:T(8,128)(2,1)} %multiply_convert_fusion, bf16[256,16,128]{0,2,1:T(8,128)(2,1)S(1)} %bitcast.69), kind=kOutput, calls=%fused_computation.5 | convolution fusion | flops 1344798720 | bytes 22020096 | tf_op jit(solution)/shard_map/hqk,qhd->khd/dot_general | solution.py:130
  297.8 14.7 %convolution_bitcast_fusion = f32[1280,16,128]{0,2,1:T(8,128)} fusion(bf16[256,16,128]{0,2,1:T(8,128)(2,1)S(1)} %copy.62, f32[16,256,1280]{1,2,0:T(8,128)} %get-tuple-element.34, f32[16,256]{1,0:T(8,128)S(1)} %log_add_fusion, pred[256,1280]{0,1:T(8,128)(4,1)S(1)} %compare_and_fusion), kind=kOutput, calls=%fused_computation.6 | convolution fusion | flops 1357905920 | bytes 32849920 | tf_op jit(solution)/shard_map/hqk,qhd->khd/dot_general | solution.py:133
  313.8 7.9 fusion.21
  321.7 3.1 copy.61
  326.1 2.9 copy.60
  330.9 2.9 copy.59
  335.7 3.0 copy.58
  340.5 3.6 collective-permute-start.9
  345.1 4.9 collective-permute-start.17
  350.0 7.8 fusion.20
  357.8 2.9 copy.68
  360.7 2.9 copy.67
  363.6 3.0 copy.66
  366.5 3.0 copy.65
  374.3 27.9 %fusion.3 = f32[1,128,2048]{2,0,1:T(1,128)S(1)} fusion(bf16[1,383,2048]{2,1,0:T(8,128)(2,1)S(1)} %maximum_bitcast_fusion.1, bf16[256,1,2048]{2,0,1:T(8,128)(2,1)S(1)} %bitcast.80), kind=kOutput, calls=%fused_computation.13 | convolution fusion | flops 134217728 | bytes 3665920 | tf_op jit(solution)/shard_map/conv_general_dilated | solution.py:50
  402.6 5.2 rev.9
  407.8 73.4 %collective-permute-start.15 = (f32[256,2048]{1,0:T(8,128)}, f32[256,2048]{1,0:T(8,128)}, u32[]{:S(2)}, u32[]{:S(2)}) collective-permute-start(f32[256,2048]{1,0:T(8,128)} %copy.67), channel_id=1, source_target_pairs={{12,0},{16,4},{20,8},{24,12},{28,16},{13,1},{17,5},{21,9},{25,13},... | collective-permute-start | bytes 6291464 | tf_op jit(solution)/shard_map/ppermute | solution.py:14
  481.2 46.8 %collective-permute-start.14 = (f32[256,2048]{1,0:T(8,128)}, f32[256,2048]{1,0:T(8,128)}, u32[]{:S(2)}, u32[]{:S(2)}) collective-permute-start(f32[256,2048]{1,0:T(8,128)} %copy.66), channel_id=1, source_target_pairs={{8,0},{12,4},{16,8},{20,12},{24,16},{28,20},{9,1},{13,5},{17,9},{2... | collective-permute-start | bytes 6291464 | tf_op jit(solution)/shard_map/ppermute | solution.py:14
  527.9 41.5 %collective-permute-done.10 = f32[256,2048]{1,0:T(8,128)} collective-permute-done((f32[256,2048]{1,0:T(8,128)}, f32[256,2048]{1,0:T(8,128)}, u32[]{:S(2)}, u32[]{:S(2)}) %collective-permute-start.10) | collective-permute-done | bytes 2097184 | tf_op jit(solution)/shard_map/ppermute | solution.py:14
  569.4 108.1 %collective-permute-start.13 = (f32[256,2048]{1,0:T(8,128)}, f32[256,2048]{1,0:T(8,128)}, u32[]{:S(2)}, u32[]{:S(2)}) collective-permute-start(f32[256,2048]{1,0:T(8,128)} %copy.64), channel_id=1, source_target_pairs={{4,0},{8,4},{12,8},{16,12},{20,16},{24,20},{28,24},{5,1},{9,5},{13... | collective-permute-start | bytes 6291464 | tf_op jit(solution)/shard_map/ppermute | solution.py:14
  677.6 30.1 %fusion.5 = f32[1,256,2048]{2,0,1:T(1,128)} fusion(bf16[1,383,2048]{2,1,0:T(8,128)(2,1)} %copy-done.13, bf16[128,1,2048]{2,0,1:T(8,128)(2,1)S(1)} %bitcast.84), kind=kOutput, calls=%fused_computation.15 | convolution fusion | flops 134217728 | bytes 4190208 | tf_op jit(solution)/shard_map/conv_general_dilated | solution.py:20
  710.0 3.3 fusion.8
  713.3 6.7 all-reduce.1
  722.9 5.5 add_convert_fusion.1
  728.4 169.9 %collective-permute-done.13 = f32[256,2048]{1,0:T(8,128)} collective-permute-done((f32[256,2048]{1,0:T(8,128)}, f32[256,2048]{1,0:T(8,128)}, u32[]{:S(2)}, u32[]{:S(2)}) %collective-permute-start.13) | collective-permute-done | bytes 2097184 | tf_op jit(solution)/shard_map/ppermute | solution.py:14
  898.3 5.3 add_convert_fusion
  (89 shorter events, 50.5 us)
Async XLA Ops:
  7.2 34.1 %copy-start.8 = (bf16[256,2048]{1,0:T(8,128)(2,1)S(1)}, bf16[256,2048]{1,0:T(8,128)(2,1)}, u32[]{:S(2)}) copy-start(bf16[256,2048]{1,0:T(8,128)(2,1)} %param.14) | copy-start | bytes 3145732
  7.2 34.1 %copy-start.14 = (bf16[256,2048]{1,0:T(8,128)(2,1)S(1)}, bf16[256,2048]{1,0:T(8,128)(2,1)}, u32[]{:S(2)}) copy-start(bf16[256,2048]{1,0:T(8,128)(2,1)} %param.11) | copy-start | bytes 3145732
  7.2 700.5 %all-reduce.4.cloned.1.call-start = ((), (), s32[]{:S(2)}) async-start(), calls=%async_computation | async-start | bytes 2097152 | tf_op jit(solution)/shard_map/psum | solution.py:151
  8.9 28.1 %copy-start.10 = (bf16[256,2048]{0,1:T(8,128)(2,1)}, bf16[256,2048]{0,1:T(8,128)(2,1)S(1)}, u32[]{:S(2)}) copy-start(bf16[256,2048]{0,1:T(8,128)(2,1)S(1)} %copy.42) | copy-start | bytes 3145732
  8.9 28.0 %collective-permute-start = (bf16[256,2048]{0,1:T(8,128)(2,1)S(1)}, bf16[256,2048]{0,1:T(8,128)(2,1)}, u32[]{:S(2)}, u32[]{:S(2)}) collective-permute-start(bf16[256,2048]{0,1:T(8,128)(2,1)S(1)} %copy.42), channel_id=1, source_target_pairs={{0,4},{4,8},{8,12},{12,16},{16,20},{20,24},{24,28},{1,5},{5,9},{9,... | collective-permute-start | bytes 3145736 | tf_op jit(solution)/shard_map/ppermute | solution.py:14
  14.6 39.0 %copy-start.16 = (s32[2048]{0:T(1024)S(1)}, s32[2048]{0:T(1024)}, u32[]{:S(2)}) copy-start(s32[2048]{0:T(1024)} %param.15) | copy-start | bytes 24580
  14.6 56.0 %collective-permute-start.5 = (bf16[256,2048]{0,1:T(8,128)(2,1)}, bf16[256,2048]{0,1:T(8,128)(2,1)}, u32[]{:S(2)}, u32[]{:S(2)}) collective-permute-start(bf16[256,2048]{0,1:T(8,128)(2,1)} %copy.48), channel_id=1, source_target_pairs={{0,4},{4,8},{8,12},{12,16},{16,20},{20,24},{24,28},{1,5},{5,9},{9,... | collective-permute-start | bytes 3145736 | tf_op jit(solution)/shard_map/ppermute | solution.py:14
  36.9 56.2 %collective-permute-start.1 = (bf16[256,2048]{0,1:T(8,128)(2,1)}, bf16[256,2048]{0,1:T(8,128)(2,1)}, u32[]{:S(2)}, u32[]{:S(2)}) collective-permute-start(bf16[256,2048]{0,1:T(8,128)(2,1)} %collective-permute-done), channel_id=1, source_target_pairs={{0,4},{4,8},{8,12},{12,16},{16,20},{20,24},{24,28},{1,5},{5,9},{9,... | collective-permute-start | bytes 3145736 | tf_op jit(solution)/shard_map/ppermute | solution.py:14
  41.7 95.2 %copy-start.3 = (bf16[256,2048]{1,0:T(8,128)(2,1)}, bf16[256,2048]{1,0:T(8,128)(2,1)S(1)}, u32[]{:S(2)}) copy-start(bf16[256,2048]{1,0:T(8,128)(2,1)S(1)} %fusion.7) | copy-start | bytes 3145732
  41.7 94.0 %collective-permute-start.4 = (bf16[127,2048]{1,0:T(8,128)(2,1)S(1)}, bf16[127,2048]{1,0:T(8,128)(2,1)}, u32[]{:S(2)}, u32[]{:S(2)}) collective-permute-start(bf16[127,2048]{1,0:T(8,128)(2,1)S(1)} %slice.88), channel_id=1, source_target_pairs={{4,0},{8,4},{12,8},{16,12},{20,16},{24,20},{28,24},{5,1},{9,5},{13... | collective-permute-start | bytes 1560584 | tf_op jit(solution)/shard_map/ppermute | solution.py:14
  43.7 100.7 %copy-start.12 = (bf16[128,2048]{1,0:T(8,128)(2,1)S(1)}, bf16[128,2048]{1,0:T(8,128)(2,1)}, u32[]{:S(2)}) copy-start(bf16[128,2048]{1,0:T(8,128)(2,1)} %param.13) | copy-start | bytes 1572868
  70.6 66.3 %collective-permute-start.6 = (bf16[256,2048]{0,1:T(8,128)(2,1)}, bf16[256,2048]{0,1:T(8,128)(2,1)S(1)}, u32[]{:S(2)}, u32[]{:S(2)}) collective-permute-start(bf16[256,2048]{0,1:T(8,128)(2,1)} %collective-permute-done.5), channel_id=1, source_target_pairs={{0,4},{4,8},{8,12},{12,16},{16,20},{20,24},{24,28},{1,5},{5,9},{9,... | collective-permute-start | bytes 3145736 | tf_op jit(solution)/shard_map/ppermute | solution.py:14
  93.1 49.3 %collective-permute-start.2 = (bf16[256,2048]{0,1:T(8,128)(2,1)}, bf16[256,2048]{0,1:T(8,128)(2,1)S(1)}, u32[]{:S(2)}, u32[]{:S(2)}) collective-permute-start(bf16[256,2048]{0,1:T(8,128)(2,1)} %collective-permute-done.1), channel_id=1, source_target_pairs={{0,4},{4,8},{8,12},{12,16},{16,20},{20,24},{24,28},{1,5},{5,9},{9,... | collective-permute-start | bytes 3145736 | tf_op jit(solution)/shard_map/ppermute | solution.py:14
  136.9 36.5 %collective-permute-start.7 = (bf16[256,2048]{0,1:T(8,128)(2,1)S(1)}, bf16[256,2048]{0,1:T(8,128)(2,1)S(1)}, u32[]{:S(2)}, u32[]{:S(2)}) collective-permute-start(bf16[256,2048]{0,1:T(8,128)(2,1)S(1)} %collective-permute-done.6), channel_id=1, source_target_pairs={{0,4},{4,8},{8,12},{12,16},{16,20},{20,24},{24,28},{1,5},{5,9},{9,... | collective-permute-start | bytes 3145736 | tf_op jit(solution)/shard_map/ppermute | solution.py:14
  142.4 46.0 %collective-permute-start.3 = (bf16[256,2048]{0,1:T(8,128)(2,1)S(1)}, bf16[256,2048]{0,1:T(8,128)(2,1)S(1)}, u32[]{:S(2)}, u32[]{:S(2)}) collective-permute-start(bf16[256,2048]{0,1:T(8,128)(2,1)S(1)} %collective-permute-done.2), channel_id=1, source_target_pairs={{0,4},{4,8},{8,12},{12,16},{16,20},{20,24},{24,28},{1,5},{5,9},{9,... | collective-permute-start | bytes 3145736 | tf_op jit(solution)/shard_map/ppermute | solution.py:14
  173.4 36.5 %collective-permute-start.8 = (bf16[256,2048]{0,1:T(8,128)(2,1)S(1)}, bf16[256,2048]{0,1:T(8,128)(2,1)S(1)}, u32[]{:S(2)}, u32[]{:S(2)}) collective-permute-start(bf16[256,2048]{0,1:T(8,128)(2,1)S(1)} %collective-permute-done.7), channel_id=1, source_target_pairs={{0,4},{4,8},{8,12},{12,16},{16,20},{20,24},{24,28},{1,5},{5,9},{9,... | collective-permute-start | bytes 3145736 | tf_op jit(solution)/shard_map/ppermute | solution.py:14
  188.5 2.8 copy-start.11
  191.3 26.6 %copy-start = (bf16[1280,2048]{0,1:T(8,128)(2,1)}, bf16[1280,2048]{0,1:T(8,128)(2,1)S(1)}, u32[]{:S(2)}) copy-start(bf16[1280,2048]{0,1:T(8,128)(2,1)S(1)} %constant_dynamic-update-slice_fusion) | copy-start | bytes 15728644
  247.9 1.0 copy-start.6
  258.7 3.1 copy-start.7
  324.8 83.0 %collective-permute-start.12 = (f32[256,2048]{1,0:T(8,128)}, f32[256,2048]{1,0:T(8,128)}, u32[]{:S(2)}, u32[]{:S(2)}) collective-permute-start(f32[256,2048]{1,0:T(8,128)} %copy.61), channel_id=1, source_target_pairs={{16,0},{20,4},{24,8},{28,12},{17,1},{21,5},{25,9},{29,13},{18,2},{... | collective-permute-start | bytes 6291464 | tf_op jit(solution)/shard_map/ppermute | solution.py:14
  329.0 152.2 %collective-permute-start.11 = (f32[256,2048]{1,0:T(8,128)}, f32[256,2048]{1,0:T(8,128)}, u32[]{:S(2)}, u32[]{:S(2)}) collective-permute-start(f32[256,2048]{1,0:T(8,128)} %copy.60), channel_id=1, source_target_pairs={{12,0},{16,4},{20,8},{24,12},{28,16},{13,1},{17,5},{21,9},{25,13},... | collective-permute-start | bytes 6291464 | tf_op jit(solution)/shard_map/ppermute | solution.py:14
  333.8 235.6 %collective-permute-start.10 = (f32[256,2048]{1,0:T(8,128)}, f32[256,2048]{1,0:T(8,128)}, u32[]{:S(2)}, u32[]{:S(2)}) collective-permute-start(f32[256,2048]{1,0:T(8,128)} %copy.59), channel_id=1, source_target_pairs={{8,0},{12,4},{16,8},{20,12},{24,16},{28,20},{9,1},{13,5},{17,9},{2... | collective-permute-start | bytes 6291464 | tf_op jit(solution)/shard_map/ppermute | solution.py:14
  338.7 5.5 copy-start.5
  340.5 382.4 %collective-permute-start.9 = (f32[256,2048]{1,0:T(8,128)}, f32[256,2048]{1,0:T(8,128)}, u32[]{:S(2)}, u32[]{:S(2)}) collective-permute-start(f32[256,2048]{1,0:T(8,128)} %copy.57), channel_id=1, source_target_pairs={{4,0},{8,4},{12,8},{16,12},{20,16},{24,20},{28,24},{5,1},{9,5},{13... | collective-permute-start | bytes 6291464 | tf_op jit(solution)/shard_map/ppermute | solution.py:14
  345.1 26.2 %collective-permute-start.17 = (bf16[127,2048]{1,0:T(8,128)(2,1)}, bf16[127,2048]{1,0:T(8,128)(2,1)}, u32[]{:S(2)}, u32[]{:S(2)}) collective-permute-start(bf16[127,2048]{1,0:T(8,128)(2,1)} %slice.99), channel_id=1, source_target_pairs={{0,4},{4,8},{8,12},{12,16},{16,20},{20,24},{24,28},{1,5},{5,9},{9,... | collective-permute-start | bytes 1560584 | tf_op jit(solution)/shard_map/ppermute | solution.py:14
  369.5 4.8 copy-start.4
  371.3 357.1 %collective-permute-start.16 = (f32[256,2048]{1,0:T(8,128)}, f32[256,2048]{1,0:T(8,128)}, u32[]{:S(2)}, u32[]{:S(2)}) collective-permute-start(f32[256,2048]{1,0:T(8,128)} %copy.68), channel_id=1, source_target_pairs={{16,0},{20,4},{24,8},{28,12},{17,1},{21,5},{25,9},{29,13},{18,2},{... | collective-permute-start | bytes 6291464 | tf_op jit(solution)/shard_map/ppermute | solution.py:14
  374.3 28.0 %copy-start.13 = (bf16[1,383,2048]{2,1,0:T(8,128)(2,1)}, bf16[1,383,2048]{2,1,0:T(8,128)(2,1)S(1)}, u32[]{:S(2)}) copy-start(bf16[1,383,2048]{2,1,0:T(8,128)(2,1)S(1)} %maximum_bitcast_fusion.1) | copy-start | bytes 4706308
  402.6 275.0 %copy-start.15 = (bf16[128,2048]{1,0:T(8,128)(2,1)S(1)}, bf16[128,2048]{1,0:T(8,128)(2,1)}, u32[]{:S(2)}) copy-start(bf16[128,2048]{1,0:T(8,128)(2,1)} %rev.8) | copy-start | bytes 1572868
  407.8 320.6 %collective-permute-start.15 = (f32[256,2048]{1,0:T(8,128)}, f32[256,2048]{1,0:T(8,128)}, u32[]{:S(2)}, u32[]{:S(2)}) collective-permute-start(f32[256,2048]{1,0:T(8,128)} %copy.67), channel_id=1, source_target_pairs={{12,0},{16,4},{20,8},{24,12},{28,16},{13,1},{17,5},{21,9},{25,13},... | collective-permute-start | bytes 6291464 | tf_op jit(solution)/shard_map/ppermute | solution.py:14
  481.2 247.2 %collective-permute-start.14 = (f32[256,2048]{1,0:T(8,128)}, f32[256,2048]{1,0:T(8,128)}, u32[]{:S(2)}, u32[]{:S(2)}) collective-permute-start(f32[256,2048]{1,0:T(8,128)} %copy.66), channel_id=1, source_target_pairs={{8,0},{12,4},{16,8},{20,12},{24,16},{28,20},{9,1},{13,5},{17,9},{2... | collective-permute-start | bytes 6291464 | tf_op jit(solution)/shard_map/ppermute | solution.py:14
  569.4 328.8 %collective-permute-start.13 = (f32[256,2048]{1,0:T(8,128)}, f32[256,2048]{1,0:T(8,128)}, u32[]{:S(2)}, u32[]{:S(2)}) collective-permute-start(f32[256,2048]{1,0:T(8,128)} %copy.64), channel_id=1, source_target_pairs={{4,0},{8,4},{12,8},{16,12},{20,16},{24,20},{28,24},{5,1},{9,5},{13... | collective-permute-start | bytes 6291464 | tf_op jit(solution)/shard_map/ppermute | solution.py:14
  677.6 32.4 %copy-start.9 = (bf16[256,2048]{1,0:T(8,128)(2,1)S(1)}, bf16[256,2048]{1,0:T(8,128)(2,1)}, u32[]{:S(2)}) copy-start(bf16[256,2048]{1,0:T(8,128)(2,1)} %param.14) | copy-start | bytes 3145732
  707.7 15.2 %copy-start.1 = (f32[256,2048]{1,0:T(8,128)S(1)}, f32[256,2048]{1,0:T(8,128)}, u32[]{:S(2)}) copy-start(f32[256,2048]{1,0:T(8,128)} %copy.58) | copy-start | bytes 6291460
  722.9 175.3 %copy-start.2 = (f32[256,2048]{1,0:T(8,128)S(1)}, f32[256,2048]{1,0:T(8,128)}, u32[]{:S(2)}) copy-start(f32[256,2048]{1,0:T(8,128)} %copy.65) | copy-start | bytes 6291460
Sparse Core Ops, SparseCore 0:
  407.9 256.6 all-reduce.3
where the time goes:
time: 917 us; the launch traced here: 911 us
  waiting for transfers between devices  333 us (36%)
  starting transfers between devices  274 us (30%)
  matrix products  157 us (17%)
  local copies, waits for them, and re-layouts  82.5 us (9%)
  other arithmetic  41.4 us (5%)
  between operations  16.4 us (2%)
    ppermute x18, waiting for transfers between devices, from_behind(): return lax.ppermute(array, axis, pairs)  333 us
    ppermute x18, starting transfers between devices, from_behind(): return lax.ppermute(array, axis, pairs)  274 us
    conv_general_dilated x1, matrix products, causal_conv(): lax.conv_general_dilated(extended[None], kernel, (1,), 'VALID', dimension...  30.1 us
    conv_general_dilated x1, matrix products, anti_conv(): lax.conv_general_dilated(extended[None], kernel, (1,), 'VALID', dimension...  29.1 us
    conv_general_dilated x1, matrix products, filter_corr(): lax.conv_general_dilated(extended[None], kernel, (1,), 'VALID', dimension...  27.9 us
    slice x5, local copies, waits for them, and re-layouts, per_device(): key_terms[first_row:first_row + shard_len]  18.6 us
    unnamed x48, local copies, waits for them, and re-layouts  18.4 us
    slice x5, local copies, waits for them, and re-layouts, per_device(): value_terms[first_row:first_row + shard_len]  18.4 us
  transfers between devices with their start and end apart: 19, of which 8 were waited for; matrix products, arithmetic and copies ran while one was open for 17% of the time, Pallas kernels for 0%

commit v1 on v0

v1 whole, which is shorter than its diff:
```python
import functools
import jax
import jax.numpy as jnp
from jax import lax
from jax.experimental import pallas as pl
from jax.experimental.pallas import tpu as pltpu
from jax.sharding import PartitionSpec as P

HD = 128
TAPS = 128
SPAN = 4
CHUNKS = 2
VMEM = 40 * 1024 * 1024


def from_behind(array, axis, by):
    size = lax.axis_size(axis)
    pairs = [(i, i + by) for i in range(size) if 0 <= i + by < size]
    return lax.ppermute(array, axis, pairs)


def causal_conv(extended, weights_in):
    channels = extended.shape[1]
    kernel = weights_in[:, None, :]
    result = lax.conv_general_dilated(
        extended[None],
        kernel,
        (1,),
        "VALID",
        dimension_numbers=("NWC", "WIO", "NWC"),
        feature_group_count=channels,
        preferred_element_type=jnp.float32,
    )
    return result[0]


def anti_conv(extended, weights_in):
    channels = extended.shape[1]
    kernel = weights_in[:, None, :]
    result = lax.conv_general_dilated(
        extended[None],
        kernel,
        (1,),
        "VALID",
        dimension_numbers=("NWC", "WIO", "NWC"),
        feature_group_count=channels,
        preferred_element_type=jnp.float32,
    )
    return result[0]


def filter_corr(extended, gradient):
    channels = extended.shape[1]
    kernel = gradient[:, None, :]
    result = lax.conv_general_dilated(
        extended[None],
        kernel,
        (1,),
        "VALID",
        dimension_numbers=("NWC", "WIO", "NWC"),
        feature_group_count=channels,
        preferred_element_type=jnp.float32,
    )
    return result[0]


def exchange(array):
    size = lax.axis_size("seq")
    return lax.ppermute(array, "seq", [(i, i ^ 1) for i in range(size)])


def dot(a, b, dims):
    return lax.dot_general(a, b, (dims, ((), ())), preferred_element_type=jnp.float32)


def attention_kernel(*refs):
    bias, queries, key_branch, mixed_grad = refs[:4]
    keys, values = refs[4 : 5 + SPAN], refs[5 + SPAN : 6 + 2 * SPAN]
    mixed_out, branch_out, query_out, own_out = refs[6 + 2 * SPAN : 10 + 2 * SPAN]
    earlier_out = refs[10 + 2 * SPAN :]
    rows = queries.shape[0]
    scale = HD ** (-0.5)
    factor = scale * 1.4426950408889634
    q = queries[...]
    scores = [
        dot(q, keys[i][...], ((1,), (1,))) * factor + bias[:, i * rows : (i + 1) * rows]
        for i in range(SPAN + 1)
    ]
    top = functools.reduce(jnp.maximum, scores)
    top = jnp.max(top, -1, keepdims=True)
    powers = [jnp.exp2(part - top) for part in scores]
    total = jnp.sum(functools.reduce(jnp.add, powers), -1, keepdims=True)
    inverse = 1.0 / total
    weights = [part * inverse for part in powers]
    probs = [part.astype(jnp.bfloat16) for part in weights]
    out = functools.reduce(
        jnp.add, [dot(probs[i], values[i][...], ((1,), (0,))) for i in range(SPAN + 1)]
    )
    out = out.astype(jnp.bfloat16).astype(jnp.float32)
    branch = key_branch[...].astype(jnp.float32)
    grad = mixed_grad[...]
    mixed_out[...] = (branch * out).astype(jnp.bfloat16)
    branch_out[...] = (grad * out).astype(jnp.bfloat16)
    attn_grad = (grad * branch).astype(jnp.bfloat16)
    row_dot = jnp.sum(attn_grad.astype(jnp.float32) * out, -1, keepdims=True)
    query_sum = None
    for i in range(SPAN + 1):
        prob_grad = dot(attn_grad, values[i][...], ((1,), (1,)))
        score_grad = (weights[i] * (prob_grad - row_dot)).astype(jnp.bfloat16)
        part = dot(score_grad, keys[i][...], ((1,), (0,)))
        query_sum = part if query_sum is None else query_sum + part
        target = own_out if i == SPAN else earlier_out[i]
        target[:, :HD] = (dot(score_grad, q, ((0,), (0,))) * scale).astype(target.dtype)
        target[:, HD:] = dot(probs[i], attn_grad, ((0,), (0,))).astype(target.dtype)
    query_out[...] = (query_sum * scale).astype(jnp.bfloat16)


def attention(bias, queries, key_branch, mixed_grad, keys_in, values_in, windows, chunk, heads):
    rows = queries.shape[0]
    width = heads * HD
    whole = pl.BlockSpec((rows, HD), lambda h: (0, chunk * heads + h))
    first = pl.BlockSpec((rows, HD), lambda h: (0, h))
    second = pl.BlockSpec((rows, HD), lambda h: (0, heads + h))
    pair = pl.BlockSpec((rows, 2 * HD), lambda h: (0, h))
    half = jax.ShapeDtypeStruct((rows, width), jnp.bfloat16)
    window = (SPAN + 1) * rows
    return pl.pallas_call(
        attention_kernel,
        grid=(heads,),
        in_specs=[pl.BlockSpec((rows, window), lambda h: (0, 0)), whole, whole, whole]
        + [first] * SPAN
        + [whole]
        + [second] * SPAN
        + [whole],
        out_specs=[first, first, first] + [pair] * (SPAN + 1),
        out_shape=[half, half, half, jax.ShapeDtypeStruct((rows, 2 * width), jnp.float32)]
        + [jax.ShapeDtypeStruct((rows, 2 * width), jnp.bfloat16)] * SPAN,
        compiler_params=pltpu.CompilerParams(vmem_limit_bytes=VMEM),
        cost_estimate=pl.CostEstimate(
            flops=heads * 24 * rows * window * HD,
            bytes_accessed=rows * width * 60,
            transcendentals=heads * rows * window,
        ),
    )(bias, queries, key_branch, mixed_grad, *windows, keys_in, *windows, values_in)


def last_sum_kernel(own, far, near, odd, key_out, value_out):
    partner = jnp.where(odd[...] == 0, near[...].astype(jnp.float32), 0.0)
    total = own[...] + far[...].astype(jnp.float32) + partner
    key_out[...] = total[:, :HD].astype(jnp.bfloat16)
    value_out[...] = total[:, HD:].astype(jnp.bfloat16)


def last_sum(own, far, near, odd):
    rows, width = own.shape[0], own.shape[1] // 2
    pair = pl.BlockSpec((rows, 2 * HD), lambda h: (0, h))
    single = pl.BlockSpec((rows, HD), lambda h: (0, h))
    flag = jnp.broadcast_to(odd, (1, 2 * HD)).astype(jnp.int32)
    return pl.pallas_call(
        last_sum_kernel,
        grid=(width // HD,),
        in_specs=[pair, pair, pair, pl.BlockSpec((1, 2 * HD), lambda h: (0, 0))],
        out_specs=[single, single],
        out_shape=[jax.ShapeDtypeStruct((rows, width), jnp.bfloat16)] * 2,
    )(own, far, near, flag)


def per_device(
    queries_in, keys_in, values_in, gate_branch, key_branch, mr_filter, out_grad, doc_ids
):
    shard_len = queries_in.shape[0]
    width = queries_in.shape[1]
    heads_dev = width // HD
    heads = heads_dev // CHUNKS
    span_cols = heads * HD
    window = (SPAN + 1) * shard_len
    position = lax.axis_index("seq")
    odd = position % 2
    f32 = jnp.float32

    windows = []
    for chunk in range(CHUNKS):
        cols = slice(chunk * span_cols, (chunk + 1) * span_cols)
        own = jnp.concatenate([keys_in[:, cols], values_in[:, cols]], 1)
        two = from_behind(own, "seq", 2)
        one = exchange(jnp.where(odd == 1, two, own))
        four = from_behind(two, "seq", 2)
        three = exchange(jnp.where(odd == 1, four, two))
        windows.append([four, three, two, one])

    doc_front = jnp.concatenate([jnp.full((SPAN * shard_len,), -1, jnp.int32), doc_ids], 0)
    key_doc = lax.dynamic_slice_in_dim(doc_front, position * shard_len, window, 0)
    query_doc = lax.dynamic_slice_in_dim(doc_ids, position * shard_len, shard_len, 0)
    query_pos = jnp.arange(shard_len, dtype=jnp.int32)
    key_pos = jnp.arange(window, dtype=jnp.int32) - SPAN * shard_len
    allowed = (query_doc[:, None] == key_doc[None, :]) & (key_pos[None, :] <= query_pos[:, None])
    bias = jnp.where(allowed, 0.0, -jnp.inf).astype(f32)

    conv_grad = (out_grad.astype(f32) * gate_branch.astype(f32)).astype(jnp.bfloat16)
    grad_edge = from_behind(conv_grad[: TAPS - 1], "seq", -1)
    mixed_grad = anti_conv(jnp.concatenate([conv_grad, grad_edge], 0), mr_filter)
    taps = jnp.arange(TAPS, dtype=jnp.int32)
    mirror = (taps[:, None] + taps[None, :] == TAPS - 1).astype(jnp.bfloat16)
    flipped = jnp.dot(mirror, mr_filter, preferred_element_type=jnp.bfloat16)

    mixed_parts, branch_parts, query_parts, key_parts, value_parts = [], [], [], [], []
    for chunk in range(CHUNKS):
        mixed_c, branch_c, query_c, own_t, t4, t3, t2, t1 = attention(
            bias, queries_in, key_branch, mixed_grad, keys_in, values_in, windows[chunk], chunk, heads
        )
        mixed_parts.append(mixed_c)
        branch_parts.append(branch_c)
        query_parts.append(query_c)
        e3 = exchange(t3)
        e1 = exchange(t1)
        s4 = (t4.astype(f32) + jnp.where(odd == 1, e3.astype(f32), 0.0)).astype(jnp.bfloat16)
        g4 = from_behind(s4, "seq", -2)
        s2 = (
            t2.astype(f32) + g4.astype(f32) + jnp.where(odd == 1, e1, e3).astype(f32)
        ).astype(jnp.bfloat16)
        g2 = from_behind(s2, "seq", -2)
        key_c, value_c = last_sum(own_t, g2, e1, odd)
        key_parts.append(key_c)
        value_parts.append(value_c)

    mixed = jnp.concatenate(mixed_parts, 1)
    mixed_edge = from_behind(mixed[shard_len - (TAPS - 1) :], "seq", 1)
    mixed_ext = jnp.concatenate([mixed_edge, mixed], 0)
    filter_part = filter_corr(mixed_ext, conv_grad)
    size = lax.axis_size("seq")
    tap_rows = TAPS // size
    blocks = jnp.concatenate(
        [filter_part[(size - 1 - j) * tap_rows : (size - j) * tap_rows][None] for j in range(size)], 0
    )
    received = lax.all_to_all(blocks, "seq", 0, 0)
    own_grad = jnp.flip(jnp.sum(received, 0), 0)
    conv_out = causal_conv(mixed_ext, flipped)
    gate_grad = (out_grad.astype(f32) * conv_out).astype(jnp.bfloat16)
    own_taps = lax.dynamic_slice_in_dim(mr_filter, position * tap_rows, tap_rows, 0).astype(f32)
    norms = lax.psum((jnp.sum(own_taps * own_taps), jnp.sum(own_grad * own_grad)), ("seq", "ch"))
    trust = jnp.sqrt(norms[0]) / jnp.sqrt(norms[1] + 1e-06)
    return (
        jnp.concatenate(query_parts, 1),
        jnp.concatenate(key_parts, 1),
        jnp.concatenate(value_parts, 1),
        gate_grad,
        jnp.concatenate(branch_parts, 1),
        trust * own_grad,
    )


def solution(mesh):
    return jax.shard_map(
        per_device,
        mesh=mesh,
        in_specs=(
            P("seq", "ch"),
            P("seq", "ch"),
            P("seq", "ch"),
            P("seq", "ch"),
            P("seq", "ch"),
            P(None, "ch"),
            P("seq", "ch"),
            P(),
        ),
        out_specs=(
            P("seq", "ch"),
            P("seq", "ch"),
            P("seq", "ch"),
            P("seq", "ch"),
            P("seq", "ch"),
            P("seq", "ch"),
        ),
        check_vma=False,
    )
```

time: 917 us -> 440 us (0.48)
  starting transfers between devices: 274 us -> 43.2 us
  waiting for transfers between devices: 333 us -> 138 us
  matrix products: 157 us -> 86.2 us
  local copies, waits for them, and re-layouts: 82.5 us -> 20.7 us
  Pallas kernels: 0 us -> 61.4 us
  blocking collectives: 6.68 us -> 57.1 us
  between operations: 16.4 us -> 2.59 us
  other arithmetic: 41.4 us -> 29.9 us
    ppermute x18 -> x10, waiting for transfers between devices: 333 us -> 71.9 us  [from_behind(): return lax.ppermute(array, axis, pairs)]
    ppermute x18 -> x10, starting transfers between devices: 274 us -> 28.8 us  [from_behind(): return lax.ppermute(array, axis, pairs)]
    dot_general x6 -> x1, matrix products: 70 us -> 1.08 us  [per_device(): flipped = jnp.dot(mirror, mr_filter, preferred_element_type=jnp.bfloat16)]
    ppermute x0 -> x8, waiting for transfers between devices: none -> 65.7 us  [exchange(): return lax.ppermute(array, 'seq', [(i, i ^ 1) for i in range(size)])]
    pallas_call x0 -> x4, Pallas kernels: none -> 61.4 us  [the longest x2 49.6 us: attention(): pl.pallas_call(attention_kernel, grid=(heads,), in_specs=[pl.BlockSpec((r...]
    psum x1, blocking collectives: 6.68 us -> 57.1 us  [per_device(): lax.psum((jnp.sum(own_taps * own_taps), jnp.sum(own_grad * own_grad)), ('...]
    slice x12 -> x2, local copies, waits for them, and re-layouts: 42.9 us -> 2.56 us  [the longest x1 1.74 us: per_device(): own = jnp.concatenate([keys_in[:, cols], values_in[:, cols]], 1)]
    rev x2 -> x1, local copies, waits for them, and re-layouts: 13.5 us -> 0.28 us  [per_device(): own_grad = jnp.flip(jnp.sum(received, 0), 0)]
  transfers between devices with their start and end apart: 19 -> 19, of which waited for: 8 -> 8; matrix products, arithmetic and copies ran while one was open for 17% -> 28% of each run, Pallas kernels for 0% -> 7%
where the time goes in v1:
time: 440 us; the launch traced here: 439 us
  waiting for transfers between devices  138 us (31%)
  matrix products  86.2 us (20%)
  Pallas kernels  61.4 us (14%)
  blocking collectives  57.1 us (13%)
  starting transfers between devices  43.2 us (10%)
  other arithmetic  29.9 us (7%)
  local copies, waits for them, and re-layouts  20.7 us (5%)
    ppermute x10, waiting for transfers between devices, from_behind(): return lax.ppermute(array, axis, pairs)  71.9 us
    ppermute x8, waiting for transfers between devices, exchange(): return lax.ppermute(array, 'seq', [(i, i ^ 1) for i in range(size)])  65.7 us
    psum x1, blocking collectives, per_device(): lax.psum((jnp.sum(own_taps * own_taps), jnp.sum(own_grad * own_grad)), ('...  57.1 us
    pallas_call x2, Pallas kernels, attention(): pl.pallas_call(attention_kernel, grid=(heads,), in_specs=[pl.BlockSpec((r...  49.6 us
    ppermute x10, starting transfers between devices, from_behind(): return lax.ppermute(array, axis, pairs)  28.8 us
    conv_general_dilated x1, matrix products, causal_conv(): lax.conv_general_dilated(extended[None], kernel, (1,), 'VALID', dimension...  28.6 us
    conv_general_dilated x1, matrix products, anti_conv(): lax.conv_general_dilated(extended[None], kernel, (1,), 'VALID', dimension...  28.6 us
    conv_general_dilated x1, matrix products, filter_corr(): lax.conv_general_dilated(extended[None], kernel, (1,), 'VALID', dimension...  27.9 us
  transfers between devices with their start and end apart: 19, of which 8 were waited for; matrix products, arithmetic and copies ran while one was open for 28% of the time, Pallas kernels for 7%

profile of v1, /device:TPU:14, one launch (start us, length us, event | category | flops | bytes accessed | tf_op | source)
XLA Modules:
  0.0 438.7 jit_solution(14539491201873004837)
XLA Ops:
  0.6 1.7 fusion.16
  2.5 3.7 collective-permute-start.5
  7.4 3.5 collective-permute-start.1
  10.9 19.9 %collective-permute-done.5.refs_6_.refs_11_ = bf16[256,2048]{1,0:T(8,128)(2,1)S(1)} collective-permute-done((bf16[256,2048]{1,0:T(8,128)(2,1)S(1)}, bf16[256,2048]{1,0:T(8,128)(2,1)S(1)}, u32[]{:S(2)}, u32[]{:S(2)}) %collective-permute-start.5) | collective-permute-done | bytes 1048608 | tf_op jit(solution)/shard_map/ppermute | solution.py:19
  30.7 3.5 collective-permute-start.6
  36.4 2.4 collective-permute-start
  39.1 14.2 %collective-permute-done.1.refs_6_.refs_11_ = bf16[256,2048]{1,0:T(8,128)(2,1)S(1)} collective-permute-done((bf16[256,2048]{1,0:T(8,128)(2,1)}, bf16[256,2048]{1,0:T(8,128)(2,1)S(1)}, u32[]{:S(2)}, u32[]{:S(2)}) %collective-permute-start.1) | collective-permute-done | bytes 1048608 | tf_op jit(solution)/shard_map/ppermute | solution.py:19
  53.2 3.5 collective-permute-start.2
  56.7 1.3 fusion.10.refs_0_
  58.0 1.6 maximum_bitcast_fusion
  59.6 16.0 %collective-permute-done.6.refs_4_.refs_9_ = bf16[256,2048]{1,0:T(8,128)(2,1)S(1)} collective-permute-done((bf16[256,2048]{1,0:T(8,128)(2,1)S(1)}, bf16[256,2048]{1,0:T(8,128)(2,1)S(1)}, u32[]{:S(2)}, u32[]{:S(2)}) %collective-permute-start.6) | collective-permute-done | bytes 1048608 | tf_op jit(solution)/shard_map/ppermute | solution.py:19
  77.2 1.5 collective-permute-start.8
  78.7 18.4 %collective-permute-done.2.refs_4_.refs_9_ = bf16[256,2048]{1,0:T(8,128)(2,1)} collective-permute-done((bf16[256,2048]{1,0:T(8,128)(2,1)S(1)}, bf16[256,2048]{1,0:T(8,128)(2,1)}, u32[]{:S(2)}, u32[]{:S(2)}) %collective-permute-start.2) | collective-permute-done | bytes 1048608 | tf_op jit(solution)/shard_map/ppermute | solution.py:19
  97.1 1.9 broadcast_select_fusion.2
  99.1 2.0 collective-permute-start.4
  101.1 28.6 %fusion = f32[1,256,2048]{2,0,1:T(1,128)S(1)} fusion(bf16[1,383,2048]{2,1,0:T(8,128)(2,1)S(1)} %maximum_bitcast_fusion, bf16[128,1,2048]{2,0,1:T(8,128)(2,1)S(1)} %bitcast.17), kind=kOutput, calls=%fused_computation | convolution fusion | flops 134217728 | bytes 4190208 | tf_op jit(solution)/shard_map/conv_general_dilated | solution.py:40
  129.7 2.4 copy.48
  132.1 15.6 %collective-permute-done.3.refs_5_.refs_10_ = bf16[256,2048]{1,0:T(8,128)(2,1)S(1)} collective-permute-done((bf16[256,2048]{1,0:T(8,128)(2,1)S(1)}, bf16[256,2048]{1,0:T(8,128)(2,1)S(1)}, u32[]{:S(2)}, u32[]{:S(2)}) %collective-permute-start.3) | collective-permute-done | bytes 1048608 | tf_op jit(solution)/shard_map/ppermute | solution.py:69
  147.7 19.3 %collective-permute-done.4.refs_7_.refs_12_ = bf16[256,2048]{1,0:T(8,128)(2,1)S(1)} collective-permute-done((bf16[256,2048]{1,0:T(8,128)(2,1)S(1)}, bf16[256,2048]{1,0:T(8,128)(2,1)S(1)}, u32[]{:S(2)}, u32[]{:S(2)}) %collective-permute-start.4) | collective-permute-done | bytes 1048608 | tf_op jit(solution)/shard_map/ppermute | solution.py:69
  167.0 24.8 %shard_map.127 = (bf16[256,1024]{1,0:T(8,128)(2,1)S(1)}, bf16[256,1024]{1,0:T(8,128)(2,1)S(1)}, bf16[256,1024]{1,0:T(8,128)(2,1)S(1)}, f32[256,2048]{1,0:T(8,128...) custom-call(f32[256,1280]{1,0:T(8,128)} %fusion.10.refs_0_, ...), custom_call_target="tpu_custom_call" | custom-call | flops 8053063680 | bytes 15728640 | tf_op jit(solution)/shard_map/pallas_call | solution.py:127
  196.3 24.8 %shard_map.128 = (bf16[256,1024]{1,0:T(8,128)(2,1)S(1)}, bf16[256,1024]{1,0:T(8,128)(2,1)S(1)}, bf16[256,1024]{1,0:T(8,128)(2,1)S(1)}, f32[256,2048]{1,0:T(8,128...) custom-call(f32[256,1280]{1,0:T(8,128)} %fusion.10.refs_0_, ...), custom_call_target="tpu_custom_call" | custom-call | flops 8053063680 | bytes 15728640 | tf_op jit(solution)/shard_map/pallas_call | solution.py:127
  224.8 3.6 collective-permute-start.17
  229.5 1.6 multiply_reduce_fusion.1
  231.6 1.6 collective-permute-start.15
  233.6 1.6 collective-permute-start.11
  235.2 2.2 pad_maximum_fusion.2
  238.4 3.4 collective-permute-done.17
  241.8 1.3 maximum_bitcast_fusion.1
  243.2 27.9 %fusion.2 = f32[1,128,2048]{2,0,1:T(1,128)S(1)} fusion(bf16[1,383,2048]{2,1,0:T(8,128)(2,1)S(1)} %maximum_bitcast_fusion.1, bf16[256,1,2048]{2,0,1:T(8,128)(2,1)S(1)} %bitcast.14), kind=kOutput, calls=%fused_computation.4 | convolution fusion | flops 134217728 | bytes 3665920 | tf_op jit(solution)/shard_map/conv_general_dilated | solution.py:55
  272.0 2.8 concatenate.43
  274.8 1.6 copy.31
  276.4 6.2 %all-to-all-start = ((f32[8,16,2048]{2,1,0:T(8,128)}), f32[8,16,2048]{2,1,0:T(8,128)}, u32[]{:S(2)}, u32[]{:S(2)}) async-start(f32[8,16,2048]{2,1,0:T(8,128)} %copy.31), calls=%async_computation | async-start | bytes 2097152 | tf_op jit(solution)/shard_map/all_to_all | solution.py:235
  282.6 1.6 add_convert_fusion.1
  284.3 2.6 collective-permute-start.14
  286.9 30.8 %collective-permute-done.9 = bf16[256,2048]{1,0:T(8,128)(2,1)} collective-permute-done((bf16[256,2048]{1,0:T(8,128)(2,1)}, bf16[256,2048]{1,0:T(8,128)(2,1)}, u32[]{:S(2)}, u32[]{:S(2)}) %collective-permute-start.9) | collective-permute-done | bytes 1048608 | tf_op jit(solution)/shard_map/ppermute | solution.py:69
  317.7 1.6 add_convert_fusion.3
  319.3 2.1 collective-permute-start.10
  321.4 28.6 %fusion.4 = f32[1,256,2048]{2,0,1:T(1,128)S(1)} fusion(bf16[1,383,2048]{2,1,0:T(8,128)(2,1)S(1)} %copy-done.36, bf16[128,1,2048]{2,0,1:T(8,128)(2,1)S(1)} %copy-done.39), kind=kOutput, calls=%fused_computation.6 | convolution fusion | flops 134217728 | bytes 4190208 | tf_op jit(solution)/shard_map/conv_general_dilated | solution.py:25
  350.1 3.0 add_convert_fusion
  353.1 1.9 collective-permute-start.16
  355.0 2.9 add_convert_fusion.2
  357.9 2.0 collective-permute-start.12
  360.0 1.3 reduce_sum.28
  362.2 1.7 fusion.7
  363.9 57.1 %all-reduce.1 = (f32[]{:T(128)}, f32[]{:T(128)}) all-reduce(f32[]{:T(128)} %multiply_reduce_fusion.1, f32[]{:T(128)} %multiply_reduce_fusion), channel_id=1, replica_groups=mesh['seq'=8,'ch'=4] {'seq','ch'}, use_global_device_ids=true, to_apply=%region_1.2 | all-reduce | flops 2 | bytes 16 | tf_op jit(solution)/shard_map/psum | solution.py:240
  423.6 5.8 %shard_map.130 = (bf16[256,1024]{1,0:T(8,128)(2,1)}, bf16[256,1024]{1,0:T(8,128)(2,1)}) custom-call(f32[256,2048]{1,0:T(8,128)} %get-tuple-element.34.own, bf16[256,2048]{1,0:T(8,128)(2,1)} %collective-permute-done.16.far, bf16[256,2048]{1,0:T(8,128)(2,1)} %collective-permute-done.15.near, s32[1,256]{1,0:T(1,128)} %broadcast_in_dim.53.odd), custom_call_target="tpu_custom_call" | custom-call | tf_op jit(solution)/shard_map/pallas_call | solution.py:159
  429.5 6.0 %shard_map.129 = (bf16[256,1024]{1,0:T(8,128)(2,1)}, bf16[256,1024]{1,0:T(8,128)(2,1)}) custom-call(f32[256,2048]{1,0:T(8,128)} %get-tuple-element.28.own, bf16[256,2048]{1,0:T(8,128)(2,1)} %collective-permute-done.12.far, bf16[256,2048]{1,0:T(8,128)(2,1)} %collective-permute-done.11.near, s32[1,256]{1,0:T(1,128)} %broadcast_in_dim.53.odd), custom_call_target="tpu_custom_call" | custom-call | tf_op jit(solution)/shard_map/pallas_call | solution.py:159
  435.4 2.2 pad_maximum_fusion.3
  (121 shorter events, 20.5 us)
Async XLA Ops:
  2.4 5.0 %copy-start.23 = (bf16[256,1024]{1,0:T(8,128)(2,1)}, bf16[256,1024]{1,0:T(8,128)(2,1)S(1)}, u32[]{:S(2)}) copy-start(bf16[256,1024]{1,0:T(8,128)(2,1)S(1)} %get-tuple-element.58) | copy-start | bytes 1572868
  2.4 5.0 %copy-start.25 = (bf16[256,1024]{1,0:T(8,128)(2,1)}, bf16[256,1024]{1,0:T(8,128)(2,1)S(1)}, u32[]{:S(2)}) copy-start(bf16[256,1024]{1,0:T(8,128)(2,1)S(1)} %get-tuple-element.67) | copy-start | bytes 1572868
  2.4 5.0 %copy-start.27 = (bf16[256,1024]{1,0:T(8,128)(2,1)}, bf16[256,1024]{1,0:T(8,128)(2,1)S(1)}, u32[]{:S(2)}) copy-start(bf16[256,1024]{1,0:T(8,128)(2,1)S(1)} %get-tuple-element.59) | copy-start | bytes 1572868
  2.4 4.9 %copy-start.29 = (bf16[256,1024]{1,0:T(8,128)(2,1)}, bf16[256,1024]{1,0:T(8,128)(2,1)S(1)}, u32[]{:S(2)}) copy-start(bf16[256,1024]{1,0:T(8,128)(2,1)S(1)} %get-tuple-element.66) | copy-start | bytes 1572868
  2.4 31.8 %copy-start.33 = (bf16[256,2048]{1,0:T(8,128)(2,1)S(1)}, bf16[256,2048]{1,0:T(8,128)(2,1)}, u32[]{:S(2)}) copy-start(bf16[256,2048]{1,0:T(8,128)(2,1)} %param.14) | copy-start | bytes 3145732
  2.4 31.8 %copy-start.37 = (bf16[256,2048]{1,0:T(8,128)(2,1)S(1)}, bf16[256,2048]{1,0:T(8,128)(2,1)}, u32[]{:S(2)}) copy-start(bf16[256,2048]{1,0:T(8,128)(2,1)} %param.11) | copy-start | bytes 3145732
  2.5 28.2 %collective-permute-start.5 = (bf16[256,2048]{1,0:T(8,128)(2,1)S(1)}, bf16[256,2048]{1,0:T(8,128)(2,1)S(1)}, u32[]{:S(2)}, u32[]{:S(2)}) collective-permute-start(bf16[256,2048]{1,0:T(8,128)(2,1)S(1)} %pad_maximum_fusion.1), channel_id=1, source_target_pairs={{0,8},{4,12},{8,16},{12,20},{16,24},{20,28},{1,9},{5,13},{9,17},{1... | collective-permute-start | bytes 3145736 | tf_op jit(solution)/shard_map/ppermute | solution.py:19
  7.4 31.5 %copy-start.43 = (s32[2048]{0:T(1024)S(1)}, s32[2048]{0:T(1024)}, u32[]{:S(2)}) copy-start(s32[2048]{0:T(1024)} %param.15) | copy-start | bytes 24580
  7.4 45.8 %collective-permute-start.1 = (bf16[256,2048]{1,0:T(8,128)(2,1)}, bf16[256,2048]{1,0:T(8,128)(2,1)S(1)}, u32[]{:S(2)}, u32[]{:S(2)}) collective-permute-start(bf16[256,2048]{1,0:T(8,128)(2,1)} %pad_maximum_fusion), channel_id=1, source_target_pairs={{0,8},{4,12},{8,16},{12,20},{16,24},{20,28},{1,9},{5,13},{9,17},{1... | collective-permute-start | bytes 3145736 | tf_op jit(solution)/shard_map/ppermute | solution.py:19
  30.7 44.9 %collective-permute-start.6 = (bf16[256,2048]{1,0:T(8,128)(2,1)S(1)}, bf16[256,2048]{1,0:T(8,128)(2,1)S(1)}, u32[]{:S(2)}, u32[]{:S(2)}) collective-permute-start(bf16[256,2048]{1,0:T(8,128)(2,1)S(1)} %collective-permute-done.5.refs_6_.refs_11_), channel_id=1, source_target_pairs={{0,8},{4,12},{8,16},{12,20},{16,24},{20,28},{1,9},{5,13},{9,17},{1... | collective-permute-start | bytes 3145736 | tf_op jit(solution)/shard_map/ppermute | solution.py:19
  36.4 21.5 %collective-permute-start = (bf16[127,2048]{1,0:T(8,128)(2,1)}, bf16[127,2048]{1,0:T(8,128)(2,1)}, u32[]{:S(2)}, u32[]{:S(2)}) collective-permute-start(bf16[127,2048]{1,0:T(8,128)(2,1)} %slice.64), channel_id=1, source_target_pairs={{4,0},{8,4},{12,8},{16,12},{20,16},{24,20},{28,24},{5,1},{9,5},{13... | collective-permute-start | bytes 1560584 | tf_op jit(solution)/shard_map/ppermute | solution.py:19
  53.2 43.9 %collective-permute-start.2 = (bf16[256,2048]{1,0:T(8,128)(2,1)S(1)}, bf16[256,2048]{1,0:T(8,128)(2,1)}, u32[]{:S(2)}, u32[]{:S(2)}) collective-permute-start(bf16[256,2048]{1,0:T(8,128)(2,1)S(1)} %collective-permute-done.1.refs_6_.refs_11_), channel_id=1, source_target_pairs={{0,8},{4,12},{8,16},{12,20},{16,24},{20,28},{1,9},{5,13},{9,17},{1... | collective-permute-start | bytes 3145736 | tf_op jit(solution)/shard_map/ppermute | solution.py:19
  58.0 17.7 %copy-start.28 = (bf16[256,1024]{1,0:T(8,128)(2,1)S(1)}, bf16[256,1024]{1,0:T(8,128)(2,1)}, u32[]{:S(2)}) copy-start(bf16[256,1024]{1,0:T(8,128)(2,1)} %copy-done.27) | copy-start | bytes 1572868
  58.0 17.7 %copy-start.30 = (bf16[256,1024]{1,0:T(8,128)(2,1)S(1)}, bf16[256,1024]{1,0:T(8,128)(2,1)}, u32[]{:S(2)}) copy-start(bf16[256,1024]{1,0:T(8,128)(2,1)} %copy-done.29) | copy-start | bytes 1572868
  59.6 37.5 %copy-start.24 = (bf16[256,1024]{1,0:T(8,128)(2,1)S(1)}, bf16[256,1024]{1,0:T(8,128)(2,1)}, u32[]{:S(2)}) copy-start(bf16[256,1024]{1,0:T(8,128)(2,1)} %copy-done.23) | copy-start | bytes 1572868
  59.6 37.5 %copy-start.26 = (bf16[256,1024]{1,0:T(8,128)(2,1)S(1)}, bf16[256,1024]{1,0:T(8,128)(2,1)}, u32[]{:S(2)}) copy-start(bf16[256,1024]{1,0:T(8,128)(2,1)} %copy-done.25) | copy-start | bytes 1572868
  76.7 118.7 %collective-permute-start.7 = (bf16[256,2048]{1,0:T(8,128)(2,1)S(1)}, bf16[256,2048]{1,0:T(8,128)(2,1)S(1)}, u32[]{:S(2)}, u32[]{:S(2)}) collective-permute-start(bf16[256,2048]{1,0:T(8,128)(2,1)S(1)} %get-tuple-element.63), channel_id=1, source_target_pairs={{0,4},{4,0},{8,12},{12,8},{16,20},{20,16},{24,28},{28,24},{1,5},{5... | collective-permute-start | bytes 3145736 | tf_op jit(solution)/shard_map/ppermute | solution.py:69
  77.2 23.9 %copy-start.38 = (bf16[128,2048]{1,0:T(8,128)(2,1)S(1)}, bf16[128,2048]{1,0:T(8,128)(2,1)}, u32[]{:S(2)}) copy-start(bf16[128,2048]{1,0:T(8,128)(2,1)} %param.13) | copy-start | bytes 1572868
  77.2 119.1 %collective-permute-start.8 = (bf16[256,2048]{1,0:T(8,128)(2,1)S(1)}, bf16[256,2048]{1,0:T(8,128)(2,1)S(1)}, u32[]{:S(2)}, u32[]{:S(2)}) collective-permute-start(bf16[256,2048]{1,0:T(8,128)(2,1)S(1)} %get-tuple-element.62), channel_id=1, source_target_pairs={{0,4},{4,0},{8,12},{12,8},{16,20},{20,16},{24,28},{28,24},{1,5},{5... | collective-permute-start | bytes 3145736 | tf_op jit(solution)/shard_map/ppermute | solution.py:69
  99.0 48.7 %collective-permute-start.3 = (bf16[256,2048]{1,0:T(8,128)(2,1)S(1)}, bf16[256,2048]{1,0:T(8,128)(2,1)S(1)}, u32[]{:S(2)}, u32[]{:S(2)}) collective-permute-start(bf16[256,2048]{1,0:T(8,128)(2,1)S(1)} %get-tuple-element.57), channel_id=1, source_target_pairs={{0,4},{4,0},{8,12},{12,8},{16,20},{20,16},{24,28},{28,24},{1,5},{5... | collective-permute-start | bytes 3145736 | tf_op jit(solution)/shard_map/ppermute | solution.py:69
  99.1 67.9 %collective-permute-start.4 = (bf16[256,2048]{1,0:T(8,128)(2,1)S(1)}, bf16[256,2048]{1,0:T(8,128)(2,1)S(1)}, u32[]{:S(2)}, u32[]{:S(2)}) collective-permute-start(bf16[256,2048]{1,0:T(8,128)(2,1)S(1)} %get-tuple-element.56), channel_id=1, source_target_pairs={{0,4},{4,0},{8,12},{12,8},{16,20},{20,16},{24,28},{28,24},{1,5},{5... | collective-permute-start | bytes 3145736 | tf_op jit(solution)/shard_map/ppermute | solution.py:69
  129.7 37.3 %copy-start = (bf16[256,2048]{1,0:T(8,128)(2,1)S(1)}, bf16[256,2048]{1,0:T(8,128)(2,1)}, u32[]{:S(2)}) copy-start(bf16[256,2048]{1,0:T(8,128)(2,1)} %refs_8_.3) | copy-start | bytes 3145732
  129.7 37.3 %copy-start.1 = (bf16[256,2048]{1,0:T(8,128)(2,1)S(1)}, bf16[256,2048]{1,0:T(8,128)(2,1)}, u32[]{:S(2)}) copy-start(bf16[256,2048]{1,0:T(8,128)(2,1)} %refs_13_.3) | copy-start | bytes 3145732
  129.7 37.3 %copy-start.15 = (bf16[256,2048]{1,0:T(8,128)(2,1)S(1)}, bf16[256,2048]{1,0:T(8,128)(2,1)}, u32[]{:S(2)}) copy-start(bf16[256,2048]{1,0:T(8,128)(2,1)} %refs_1_.3) | copy-start | bytes 3145732
  129.7 37.3 %copy-start.16 = (bf16[256,2048]{1,0:T(8,128)(2,1)S(1)}, bf16[256,2048]{1,0:T(8,128)(2,1)}, u32[]{:S(2)}) copy-start(bf16[256,2048]{1,0:T(8,128)(2,1)} %refs_2_.3) | copy-start | bytes 3145732
  167.0 29.3 %copy-start.5 = (bf16[256,2048]{1,0:T(8,128)(2,1)S(1)}, bf16[256,2048]{1,0:T(8,128)(2,1)}, u32[]{:S(2)}) copy-start(bf16[256,2048]{1,0:T(8,128)(2,1)} %copy-done.4) | copy-start | bytes 3145732
  223.1 5.4 %copy-start.19 = (bf16[256,2048]{1,0:T(8,128)(2,1)}, bf16[256,2048]{1,0:T(8,128)(2,1)S(1)}, u32[]{:S(2)}) copy-start(bf16[256,2048]{1,0:T(8,128)(2,1)S(1)} %get-tuple-element.38) | copy-start | bytes 3145732
  223.1 12.1 %copy-start.11 = (bf16[256,1024]{1,0:T(8,128)(2,1)S(1)}, bf16[256,1024]{1,0:T(8,128)(2,1)}, u32[]{:S(2)}) copy-start(bf16[256,1024]{1,0:T(8,128)(2,1)} %copy-done.10) | copy-start | bytes 1572868
  223.9 13.5 %copy-start.9 = (bf16[256,1024]{1,0:T(8,128)(2,1)S(1)}, bf16[256,1024]{1,0:T(8,128)(2,1)}, u32[]{:S(2)}) copy-start(bf16[256,1024]{1,0:T(8,128)(2,1)} %copy-done.8) | copy-start | bytes 1572868
  224.8 17.1 %collective-permute-start.17 = (bf16[127,2048]{1,0:T(8,128)(2,1)}, bf16[127,2048]{1,0:T(8,128)(2,1)}, u32[]{:S(2)}, u32[]{:S(2)}) collective-permute-start(bf16[127,2048]{1,0:T(8,128)(2,1)} %slice.65), channel_id=1, source_target_pairs={{0,4},{4,8},{8,12},{12,16},{16,20},{20,24},{24,28},{1,5},{5,9},{9,... | collective-permute-start | bytes 1560584 | tf_op jit(solution)/shard_map/ppermute | solution.py:19
  229.5 7.9 %copy-start.13 = (bf16[256,1024]{1,0:T(8,128)(2,1)S(1)}, bf16[256,1024]{1,0:T(8,128)(2,1)}, u32[]{:S(2)}) copy-start(bf16[256,1024]{1,0:T(8,128)(2,1)} %copy-done.12) | copy-start | bytes 1572868
  231.1 51.5 %collective-permute-start.13 = (bf16[256,2048]{1,0:T(8,128)(2,1)}, bf16[256,2048]{1,0:T(8,128)(2,1)}, u32[]{:S(2)}, u32[]{:S(2)}) collective-permute-start(bf16[256,2048]{1,0:T(8,128)(2,1)} %copy-done.20), channel_id=1, source_target_pairs={{0,4},{4,0},{8,12},{12,8},{16,20},{20,16},{24,28},{28,24},{1,5},{5... | collective-permute-start | bytes 3145736 | tf_op jit(solution)/shard_map/ppermute | solution.py:69
  231.6 118.5 %collective-permute-start.15 = (bf16[256,2048]{1,0:T(8,128)(2,1)}, bf16[256,2048]{1,0:T(8,128)(2,1)}, u32[]{:S(2)}, u32[]{:S(2)}) collective-permute-start(bf16[256,2048]{1,0:T(8,128)(2,1)} %copy-done.19), channel_id=1, source_target_pairs={{0,4},{4,0},{8,12},{12,8},{16,20},{20,16},{24,28},{28,24},{1,5},{5... | collective-permute-start | bytes 3145736 | tf_op jit(solution)/shard_map/ppermute | solution.py:69
  233.1 84.5 %collective-permute-start.9 = (bf16[256,2048]{1,0:T(8,128)(2,1)}, bf16[256,2048]{1,0:T(8,128)(2,1)}, u32[]{:S(2)}, u32[]{:S(2)}) collective-permute-start(bf16[256,2048]{1,0:T(8,128)(2,1)} %copy-done.18), channel_id=1, source_target_pairs={{0,4},{4,0},{8,12},{12,8},{16,20},{20,16},{24,28},{28,24},{1,5},{5... | collective-permute-start | bytes 3145736 | tf_op jit(solution)/shard_map/ppermute | solution.py:69
  233.6 121.4 %collective-permute-start.11 = (bf16[256,2048]{1,0:T(8,128)(2,1)}, bf16[256,2048]{1,0:T(8,128)(2,1)}, u32[]{:S(2)}, u32[]{:S(2)}) collective-permute-start(bf16[256,2048]{1,0:T(8,128)(2,1)} %copy-done.17), channel_id=1, source_target_pairs={{0,4},{4,0},{8,12},{12,8},{16,20},{20,16},{24,28},{28,24},{1,5},{5... | collective-permute-start | bytes 3145736 | tf_op jit(solution)/shard_map/ppermute | solution.py:69
  235.2 6.7 %copy-start.32 = (bf16[256,2048]{1,0:T(8,128)(2,1)S(1)}, bf16[256,2048]{1,0:T(8,128)(2,1)}, u32[]{:S(2)}) copy-start(bf16[256,2048]{1,0:T(8,128)(2,1)} %copy-done.31) | copy-start | bytes 3145732
  238.4 4.8 %copy-start.22 = (bf16[256,2048]{1,0:T(8,128)(2,1)S(1)}, bf16[256,2048]{1,0:T(8,128)(2,1)}, u32[]{:S(2)}) copy-start(bf16[256,2048]{1,0:T(8,128)(2,1)} %copy-done.21) | copy-start | bytes 3145732
  243.2 28.0 %copy-start.35 = (bf16[1,383,2048]{2,1,0:T(8,128)(2,1)}, bf16[1,383,2048]{2,1,0:T(8,128)(2,1)S(1)}, u32[]{:S(2)}) copy-start(bf16[1,383,2048]{2,1,0:T(8,128)(2,1)S(1)} %maximum_bitcast_fusion.1) | copy-start | bytes 4706308
  276.4 83.6 %all-to-all-start = ((f32[8,16,2048]{2,1,0:T(8,128)}), f32[8,16,2048]{2,1,0:T(8,128)}, u32[]{:S(2)}, u32[]{:S(2)}) async-start(f32[8,16,2048]{2,1,0:T(8,128)} %copy.31), calls=%async_computation | async-start | bytes 2097152 | tf_op jit(solution)/shard_map/all_to_all | solution.py:235
  284.3 37.1 %copy-start.36 = (bf16[1,383,2048]{2,1,0:T(8,128)(2,1)S(1)}, bf16[1,383,2048]{2,1,0:T(8,128)(2,1)}, u32[]{:S(2)}) copy-start(bf16[1,383,2048]{2,1,0:T(8,128)(2,1)} %copy-done.35) | copy-start | bytes 4706308
  284.3 37.1 %copy-start.39 = (bf16[128,1,2048]{2,0,1:T(8,128)(2,1)S(1)}, bf16[128,1,2048]{2,0,1:T(8,128)(2,1)}, u32[]{:S(2)}) copy-start(bf16[128,1,2048]{2,0,1:T(8,128)(2,1)} %convolution_bitcast_fusion) | copy-start | bytes 1572868
  284.3 65.8 %collective-permute-start.14 = (bf16[256,2048]{1,0:T(8,128)(2,1)S(1)}, bf16[256,2048]{1,0:T(8,128)(2,1)S(1)}, u32[]{:S(2)}, u32[]{:S(2)}) collective-permute-start(bf16[256,2048]{1,0:T(8,128)(2,1)S(1)} %add_convert_fusion.1), channel_id=1, source_target_pairs={{8,0},{12,4},{16,8},{20,12},{24,16},{28,20},{9,1},{13,5},{17,9},{2... | collective-permute-start | bytes 3145736 | tf_op jit(solution)/shard_map/ppermute | solution.py:19
  319.3 30.8 %copy-start.7 = (bf16[256,2048]{1,0:T(8,128)(2,1)S(1)}, bf16[256,2048]{1,0:T(8,128)(2,1)}, u32[]{:S(2)}) copy-start(bf16[256,2048]{1,0:T(8,128)(2,1)} %copy-done.6) | copy-start | bytes 3145732
  319.3 35.7 %collective-permute-start.10 = (bf16[256,2048]{1,0:T(8,128)(2,1)S(1)}, bf16[256,2048]{1,0:T(8,128)(2,1)S(1)}, u32[]{:S(2)}, u32[]{:S(2)}) collective-permute-start(bf16[256,2048]{1,0:T(8,128)(2,1)S(1)} %add_convert_fusion.3), channel_id=1, source_target_pairs={{8,0},{12,4},{16,8},{20,12},{24,16},{28,20},{9,1},{13,5},{17,9},{2... | collective-permute-start | bytes 3145736 | tf_op jit(solution)/shard_map/ppermute | solution.py:19
  350.1 4.9 %copy-start.3 = (bf16[256,2048]{1,0:T(8,128)(2,1)S(1)}, bf16[256,2048]{1,0:T(8,128)(2,1)}, u32[]{:S(2)}) copy-start(bf16[256,2048]{1,0:T(8,128)(2,1)} %copy-done.2) | copy-start | bytes 3145732
  353.1 69.9 %collective-permute-start.16 = (bf16[256,2048]{1,0:T(8,128)(2,1)}, bf16[256,2048]{1,0:T(8,128)(2,1)}, u32[]{:S(2)}, u32[]{:S(2)}) collective-permute-start(bf16[256,2048]{1,0:T(8,128)(2,1)} %add_convert_fusion), channel_id=1, source_target_pairs={{8,0},{12,4},{16,8},{20,12},{24,16},{28,20},{9,1},{13,5},{17,9},{2... | collective-permute-start | bytes 3145736 | tf_op jit(solution)/shard_map/ppermute | solution.py:19
  357.9 71.5 %collective-permute-start.12 = (bf16[256,2048]{1,0:T(8,128)(2,1)}, bf16[256,2048]{1,0:T(8,128)(2,1)}, u32[]{:S(2)}, u32[]{:S(2)}) collective-permute-start(bf16[256,2048]{1,0:T(8,128)(2,1)} %add_convert_fusion.2), channel_id=1, source_target_pairs={{8,0},{12,4},{16,8},{20,12},{24,16},{28,20},{9,1},{13,5},{17,9},{2... | collective-permute-start | bytes 3145736 | tf_op jit(solution)/shard_map/ppermute | solution.py:19
  429.4 6.0 %copy-start.41 = (bf16[256,1024]{1,0:T(8,128)(2,1)S(1)}, bf16[256,1024]{1,0:T(8,128)(2,1)}, u32[]{:S(2)}) copy-start(bf16[256,1024]{1,0:T(8,128)(2,1)} %get-tuple-element.39) | copy-start | bytes 1572868
  (15 other events, 24.2 us)

commit v2 on v1

--- a/solution.py
+++ b/solution.py
@@ -10,6 +10,7 @@
 TAPS = 128
 SPAN = 4
 CHUNKS = 2
+LAST_HEADS = 4
 VMEM = 40 * 1024 * 1024
 
 
@@ -145,20 +146,23 @@
 
 
 def last_sum_kernel(own, far, near, odd, key_out, value_out):
-    partner = jnp.where(odd[...] == 0, near[...].astype(jnp.float32), 0.0)
-    total = own[...] + far[...].astype(jnp.float32) + partner
-    key_out[...] = total[:, :HD].astype(jnp.bfloat16)
-    value_out[...] = total[:, HD:].astype(jnp.bfloat16)
+    for head in range(LAST_HEADS):
+        wide = slice(head * 2 * HD, (head + 1) * 2 * HD)
+        narrow = slice(head * HD, (head + 1) * HD)
+        partner = jnp.where(odd[...] == 0, near[:, wide].astype(jnp.float32), 0.0)
+        total = own[:, wide] + far[:, wide].astype(jnp.float32) + partner
+        key_out[:, narrow] = total[:, :HD].astype(jnp.bfloat16)
+        value_out[:, narrow] = total[:, HD:].astype(jnp.bfloat16)
 
 
 def last_sum(own, far, near, odd):
     rows, width = own.shape[0], own.shape[1] // 2
-    pair = pl.BlockSpec((rows, 2 * HD), lambda h: (0, h))
-    single = pl.BlockSpec((rows, HD), lambda h: (0, h))
+    pair = pl.BlockSpec((rows, LAST_HEADS * 2 * HD), lambda h: (0, h))
+    single = pl.BlockSpec((rows, LAST_HEADS * HD), lambda h: (0, h))
     flag = jnp.broadcast_to(odd, (1, 2 * HD)).astype(jnp.int32)
     return pl.pallas_call(
         last_sum_kernel,
-        grid=(width // HD,),
+        grid=(width // (LAST_HEADS * HD),),
         in_specs=[pair, pair, pair, pl.BlockSpec((1, 2 * HD), lambda h: (0, 0))],
         out_specs=[single, single],
         out_shape=[jax.ShapeDtypeStruct((rows, width), jnp.bfloat16)] * 2,
@@ -178,15 +182,9 @@
     odd = position % 2
     f32 = jnp.float32
 
-    windows = []
-    for chunk in range(CHUNKS):
-        cols = slice(chunk * span_cols, (chunk + 1) * span_cols)
-        own = jnp.concatenate([keys_in[:, cols], values_in[:, cols]], 1)
-        two = from_behind(own, "seq", 2)
-        one = exchange(jnp.where(odd == 1, two, own))
-        four = from_behind(two, "seq", 2)
-        three = exchange(jnp.where(odd == 1, four, two))
-        windows.append([four, three, two, one])
+    columns = [slice(c * span_cols, (c + 1) * span_cols) for c in range(CHUNKS)]
+    owns = [jnp.concatenate([keys_in[:, c], values_in[:, c]], 1) for c in columns]
+    twos = [from_behind(own, "seq", 2) for own in owns]
 
     doc_front = jnp.concatenate([jnp.full((SPAN * shard_len,), -1, jnp.int32), doc_ids], 0)
     key_doc = lax.dynamic_slice_in_dim(doc_front, position * shard_len, window, 0)
@@ -203,47 +201,64 @@
     mirror = (taps[:, None] + taps[None, :] == TAPS - 1).astype(jnp.bfloat16)
     flipped = jnp.dot(mirror, mr_filter, preferred_element_type=jnp.bfloat16)
 
-    mixed_parts, branch_parts, query_parts, key_parts, value_parts = [], [], [], [], []
+    mixed_grad, bias, flipped, *twos = lax.optimization_barrier((mixed_grad, bias, flipped, *twos))
+    ones = [exchange(jnp.where(odd == 1, two, own)) for own, two in zip(owns, twos)]
+    fours = [from_behind(two, "seq", 2) for two in twos]
+    ones, fours = lax.optimization_barrier((ones, fours))
+    threes = [exchange(jnp.where(odd == 1, four, two)) for four, two in zip(fours, twos)]
+    windows = [list(window) for window in zip(fours, threes, twos, ones)]
+
+    size = lax.axis_size("seq")
+    tap_rows = TAPS // size
+    query_parts, branch_parts, gate_parts, filter_parts, sums = [], [], [], [], []
+    sources = (queries_in, key_branch, mixed_grad, keys_in, values_in, *windows[0])
     for chunk in range(CHUNKS):
-        mixed_c, branch_c, query_c, own_t, t4, t3, t2, t1 = attention(
-            bias, queries_in, key_branch, mixed_grad, keys_in, values_in, windows[chunk], chunk, heads
+        cols = columns[chunk]
+        mixed, branch_c, query_c, own_t, t4, t3, t2, t1 = attention(
+            bias, *sources[:5], sources[5:], chunk, heads
         )
-        mixed_parts.append(mixed_c)
         branch_parts.append(branch_c)
         query_parts.append(query_c)
         e3 = exchange(t3)
         e1 = exchange(t1)
+        mixed_edge = from_behind(mixed[shard_len - (TAPS - 1) :], "seq", 1)
+        mixed_ext = jnp.concatenate([mixed_edge, mixed], 0)
+        filter_part = filter_corr(mixed_ext, conv_grad[:, cols])
+        conv_out = causal_conv(mixed_ext, flipped[:, cols])
+        gate_c = (out_grad[:, cols].astype(f32) * conv_out).astype(jnp.bfloat16)
+        if chunk + 1 < CHUNKS:
+            gate_c, filter_part, e3, *rest = lax.optimization_barrier(
+                (gate_c, filter_part, e3, *sources[:5], *windows[chunk + 1])
+            )
+            sources = tuple(rest)
+        gate_parts.append(gate_c)
+        blocks = jnp.concatenate(
+            [
+                filter_part[(size - 1 - j) * tap_rows : (size - j) * tap_rows][None]
+                for j in range(size)
+            ],
+            0,
+        )
+        received = lax.all_to_all(blocks, "seq", 0, 0)
+        filter_parts.append(jnp.sum(received, 0))
         s4 = (t4.astype(f32) + jnp.where(odd == 1, e3.astype(f32), 0.0)).astype(jnp.bfloat16)
         g4 = from_behind(s4, "seq", -2)
         s2 = (
             t2.astype(f32) + g4.astype(f32) + jnp.where(odd == 1, e1, e3).astype(f32)
         ).astype(jnp.bfloat16)
         g2 = from_behind(s2, "seq", -2)
-        key_c, value_c = last_sum(own_t, g2, e1, odd)
-        key_parts.append(key_c)
-        value_parts.append(value_c)
-
-    mixed = jnp.concatenate(mixed_parts, 1)
-    mixed_edge = from_behind(mixed[shard_len - (TAPS - 1) :], "seq", 1)
-    mixed_ext = jnp.concatenate([mixed_edge, mixed], 0)
-    filter_part = filter_corr(mixed_ext, conv_grad)
-    size = lax.axis_size("seq")
-    tap_rows = TAPS // size
-    blocks = jnp.concatenate(
-        [filter_part[(size - 1 - j) * tap_rows : (size - j) * tap_rows][None] for j in range(size)], 0
-    )
-    received = lax.all_to_all(blocks, "seq", 0, 0)
-    own_grad = jnp.flip(jnp.sum(received, 0), 0)
-    conv_out = causal_conv(mixed_ext, flipped)
-    gate_grad = (out_grad.astype(f32) * conv_out).astype(jnp.bfloat16)
+        sums.append((own_t, g2, e1))
+
+    own_grad = jnp.flip(jnp.concatenate(filter_parts, 1), 0)
     own_taps = lax.dynamic_slice_in_dim(mr_filter, position * tap_rows, tap_rows, 0).astype(f32)
     norms = lax.psum((jnp.sum(own_taps * own_taps), jnp.sum(own_grad * own_grad)), ("seq", "ch"))
     trust = jnp.sqrt(norms[0]) / jnp.sqrt(norms[1] + 1e-06)
+    ends = [last_sum(*terms, odd) for terms in sums]
     return (
         jnp.concatenate(query_parts, 1),
-        jnp.concatenate(key_parts, 1),
-        jnp.concatenate(value_parts, 1),
-        gate_grad,
+        jnp.concatenate([end[0] for end in ends], 1),
+        jnp.concatenate([end[1] for end in ends], 1),
+        jnp.concatenate(gate_parts, 1),
         jnp.concatenate(branch_parts, 1),
         trust * own_grad,
     )

time: 440 us -> 411 us (0.934)
  waiting for transfers between devices: 138 us -> 90.3 us
  local copies, waits for them, and re-layouts: 20.7 us -> 36.7 us
  starting transfers between devices: 43.2 us -> 50.7 us
  blocking collectives: 57.1 us -> 51.7 us
  Pallas kernels: 61.4 us -> 56.1 us
    ppermute x10 -> x11, waiting for transfers between devices: 71.9 us -> 17.8 us  [from_behind(): return lax.ppermute(array, axis, pairs)]
    unnamed x90 -> x117, local copies, waits for them, and re-layouts: 11 us -> 23.5 us
    ppermute x8, waiting for transfers between devices: 65.7 us -> 72.6 us  [exchange(): return lax.ppermute(array, 'seq', [(i, i ^ 1) for i in range(size)])]
    psum x1, blocking collectives: 57.1 us -> 51.7 us  [per_device(): lax.psum((jnp.sum(own_taps * own_taps), jnp.sum(own_grad * own_grad)), ('...]
    all_to_all x1 -> x2, starting transfers between devices: 6.22 us -> 11.5 us  [per_device(): received = lax.all_to_all(blocks, 'seq', 0, 0)]
    pallas_call x2, Pallas kernels: 11.8 us -> 6.54 us  [last_sum(): pl.pallas_call(last_sum_kernel, grid=(width // (LAST_HEADS * HD),), in_sp...]
    ppermute x10 -> x11, starting transfers between devices: 28.8 us -> 32.1 us  [from_behind(): return lax.ppermute(array, axis, pairs)]
    conv_general_dilated x1 -> x2, matrix products: 28.6 us -> 29.4 us  [causal_conv(): lax.conv_general_dilated(extended[None], kernel, (1,), 'VALID', dimension...]
  transfers between devices with their start and end apart: 19 -> 21, of which waited for: 8 -> 8; matrix products, arithmetic and copies ran while one was open for 28% -> 32% of each run, Pallas kernels for 7% -> 7%
where the time goes in v2:
time: 411 us; the launch traced here: 407 us
  waiting for transfers between devices  90.3 us (22%)
  matrix products  87.9 us (21%)
  Pallas kernels  56.1 us (14%)
  blocking collectives  51.7 us (13%)
  starting transfers between devices  50.7 us (12%)
  local copies, waits for them, and re-layouts  36.7 us (9%)
  other arithmetic  30.5 us (7%)
    ppermute x8, waiting for transfers between devices, exchange(): return lax.ppermute(array, 'seq', [(i, i ^ 1) for i in range(size)])  72.6 us
    psum x1, blocking collectives, per_device(): lax.psum((jnp.sum(own_taps * own_taps), jnp.sum(own_grad * own_grad)), ('...  51.7 us
    pallas_call x2, Pallas kernels, attention(): pl.pallas_call(attention_kernel, grid=(heads,), in_specs=[pl.BlockSpec((r...  49.6 us
    ppermute x11, starting transfers between devices, from_behind(): return lax.ppermute(array, axis, pairs)  32.1 us
    conv_general_dilated x2, matrix products, causal_conv(): lax.conv_general_dilated(extended[None], kernel, (1,), 'VALID', dimension...  29.4 us
    conv_general_dilated x1, matrix products, anti_conv(): lax.conv_general_dilated(extended[None], kernel, (1,), 'VALID', dimension...  28.6 us
    conv_general_dilated x2, matrix products, filter_corr(): lax.conv_general_dilated(extended[None], kernel, (1,), 'VALID', dimension...  27.8 us
    unnamed x117, local copies, waits for them, and re-layouts  23.5 us
  transfers between devices with their start and end apart: 21, of which 8 were waited for; matrix products, arithmetic and copies ran while one was open for 32% of the time, Pallas kernels for 7%

profile of v2, /device:TPU:14, one launch (start us, length us, event | category | flops | bytes accessed | tf_op | source)
XLA Modules:
  0.0 406.7 jit_solution(7139293782622413612)
XLA Ops:
  0.6 1.7 fusion.22
  3.5 3.6 collective-permute-start.1
  8.2 3.5 collective-permute-start.2
  13.1 2.4 collective-permute-start
  15.5 2.1 fusion.19
  17.8 1.3 fusion.3.refs_0_
  19.2 10.1 %collective-permute-done = bf16[127,2048]{1,0:T(8,128)(2,1)} collective-permute-done((bf16[127,2048]{1,0:T(8,128)(2,1)}, bf16[127,2048]{1,0:T(8,128)(2,1)}, u32[]{:S(2)}, u32[]{:S(2)}) %collective-permute-start) | collective-permute-done | bytes 520224 | tf_op jit(solution)/shard_map/ppermute | solution.py:20
  30.4 28.6 %fusion = f32[1,256,2048]{2,0,1:T(1,128)S(1)} fusion(bf16[1,383,2048]{2,1,0:T(8,128)(2,1)S(1)} %maximum_bitcast_fusion, bf16[128,1,2048]{2,0,1:T(8,128)(2,1)S(1)} %bitcast.56), kind=kOutput, calls=%fused_computation | convolution fusion | flops 134217728 | bytes 4190208 | tf_op jit(solution)/shard_map/conv_general_dilated | solution.py:41
  59.1 2.2 copy.90
  62.9 1.4 collective-permute-start.3
  64.3 2.2 collective-permute-start.5
  66.5 1.9 collective-permute-start.6
  68.5 19.5 %collective-permute-done.4.refs_7_.refs_12_ = bf16[256,2048]{1,0:T(8,128)(2,1)S(1)} collective-permute-done((bf16[256,2048]{1,0:T(8,128)(2,1)S(1)}, bf16[256,2048]{1,0:T(8,128)(2,1)S(1)}, u32[]{:S(2)}, u32[]{:S(2)}) %collective-permute-start.4) | collective-permute-done | bytes 1048608 | tf_op jit(solution)/shard_map/ppermute | solution.py:70
  87.9 19.8 %collective-permute-done.3.refs_7_.refs_12_ = bf16[256,2048]{1,0:T(8,128)(2,1)S(1)} collective-permute-done((bf16[256,2048]{1,0:T(8,128)(2,1)S(1)}, bf16[256,2048]{1,0:T(8,128)(2,1)S(1)}, u32[]{:S(2)}, u32[]{:S(2)}) %collective-permute-start.3) | collective-permute-done | bytes 1048608 | tf_op jit(solution)/shard_map/ppermute | solution.py:70
  108.7 2.8 collective-permute-done.6.refs_4_.refs_9_
  114.6 1.7 multiply_reduce_fusion.1
  116.3 2.1 slice_bitcast_fusion
  118.3 1.8 slice_bitcast_fusion.2
  120.1 15.8 %collective-permute-done.7.refs_5_.refs_10_ = bf16[256,2048]{1,0:T(8,128)(2,1)} collective-permute-done((bf16[256,2048]{1,0:T(8,128)(2,1)}, bf16[256,2048]{1,0:T(8,128)(2,1)}, u32[]{:S(2)}, u32[]{:S(2)}) %collective-permute-start.7) | collective-permute-done | bytes 1048608 | tf_op jit(solution)/shard_map/ppermute | solution.py:70
  139.6 24.7 %shard_map.127 = (bf16[256,1024]{1,0:T(8,128)(2,1)S(1)}, bf16[256,1024]{1,0:T(8,128)(2,1)S(1)}, bf16[256,1024]{1,0:T(8,128)(2,1)S(1)}, f32[256,2048]{1,0:T(8,128...) custom-call(f32[256,1280]{1,0:T(8,128)} %fusion.3.refs_0_, ...), custom_call_target="tpu_custom_call" | custom-call | flops 8053063680 | bytes 15728640 | tf_op jit(solution)/shard_map/pallas_call | solution.py:128
  164.3 3.7 collective-permute-start.8
  168.6 1.6 collective-permute-start.9
  170.7 4.8 %collective-permute-done.8 = bf16[127,1024]{1,0:T(8,128)(2,1)S(1)} collective-permute-done((bf16[127,1024]{1,0:T(8,128)(2,1)S(1)}, bf16[127,1024]{1,0:T(8,128)(2,1)S(1)}, u32[]{:S(2)}, u32[]{:S(2)}) %collective-permute-start.8) | collective-permute-done | bytes 260128 | tf_op jit(solution)/shard_map/ppermute | solution.py:20
  175.6 13.9 %fusion.8 = f32[1,128,1024]{2,0,1:T(1,128)S(1)} fusion(bf16[1,383,1024]{2,1,0:T(8,128)(2,1)S(1)} %maximum_bitcast_fusion.1, bf16[256,1,1024]{2,0,1:T(8,128)(2,1)S(1)} %get-tuple-element.91), kind=kOutput, calls=%fused_computation.16 | convolution fusion | flops 67108864 | bytes 1832960 | tf_op jit(solution)/shard_map/conv_general_dilated | solution.py:56
  189.6 14.2 %fusion.10 = f32[1,256,1024]{2,0,1:T(1,128)S(1)} fusion(bf16[1,383,1024]{2,1,0:T(8,128)(2,1)S(1)} %maximum_bitcast_fusion.1, bf16[128,1,1024]{2,0,1:T(8,128)(2,1)S(1)} %get-tuple-element.105), kind=kOutput, calls=%fused_computation.18 | convolution fusion | flops 67108864 | bytes 2095104 | tf_op jit(solution)/shard_map/conv_general_dilated | solution.py:26
  205.9 14.5 %collective-permute-done.9 = bf16[256,2048]{1,0:T(8,128)(2,1)S(1)} collective-permute-done((bf16[256,2048]{1,0:T(8,128)(2,1)S(1)}, bf16[256,2048]{1,0:T(8,128)(2,1)S(1)}, u32[]{:S(2)}, u32[]{:S(2)}) %collective-permute-start.9) | collective-permute-done | bytes 1048608 | tf_op jit(solution)/shard_map/ppermute | solution.py:70
  226.5 4.5 %all-to-all-start = ((f32[8,16,1024]{2,1,0:T(8,128)}), f32[8,16,1024]{2,1,0:T(8,128)}, u32[]{:S(2)}, u32[]{:S(2)}) async-start(f32[8,16,1024]{2,1,0:T(8,128)} %bitcast_dynamic-update-slice_fusion), calls=%async_computation | async-start | bytes 1048576 | tf_op jit(solution)/shard_map/all_to_all | solution.py:242
  238.4 24.9 %shard_map.128 = (bf16[256,1024]{1,0:T(8,128)(2,1)S(1)}, bf16[256,1024]{1,0:T(8,128)(2,1)S(1)}, bf16[256,1024]{1,0:T(8,128)(2,1)S(1)}, f32[256,2048]{1,0:T(8,128...) custom-call(f32[256,1280]{1,0:T(8,128)} %fusion.3.refs_0_, ...), custom_call_target="tpu_custom_call" | custom-call | flops 8053063680 | bytes 15728640 | tf_op jit(solution)/shard_map/pallas_call | solution.py:128
  263.3 3.5 collective-permute-start.18
  266.9 1.4 add_convert_fusion.3
  268.3 2.5 collective-permute-start.11
  271.4 1.4 collective-permute-start.16
  275.1 13.9 %fusion.4 = f32[1,128,1024]{2,0,1:T(1,128)S(1)} fusion(bf16[1,383,1024]{2,1,0:T(8,128)(2,1)S(1)} %maximum_bitcast_fusion.2, bf16[256,1,1024]{2,0,1:T(8,128)(2,1)S(1)} %copy-done.48), kind=kOutput, calls=%fused_computation.12 | convolution fusion | flops 67108864 | bytes 1832960 | tf_op jit(solution)/shard_map/conv_general_dilated | solution.py:56
  289.7 2.2 concatenate.54
  291.9 2.1 copy.61
  294.1 3.0 collective-permute-done.14
  297.1 1.4 add_convert_fusion.1
  298.4 2.5 collective-permute-start.15
  300.9 7.0 %all-to-all-start.1 = ((f32[8,16,1024]{2,1,0:T(8,128)}), f32[8,16,1024]{2,1,0:T(8,128)}, u32[]{:S(2)}, u32[]{:S(2)}) async-start(f32[8,16,1024]{2,1,0:T(8,128)} %copy.61), calls=%async_computation.1 | async-start | bytes 1048576 | tf_op jit(solution)/shard_map/all_to_all | solution.py:242
  307.9 15.2 %fusion.6 = f32[1,256,1024]{2,0,1:T(1,128)S(1)} fusion(bf16[1,383,1024]{2,1,0:T(8,128)(2,1)} %copy-done.46, bf16[128,1,1024]{2,0,1:T(8,128)(2,1)S(1)} %copy-done.52), kind=kOutput, calls=%fused_computation.14 | convolution fusion | flops 67108864 | bytes 2095104 | tf_op jit(solution)/shard_map/conv_general_dilated | solution.py:26
  325.3 3.4 add_convert_fusion.2
  328.7 2.5 collective-permute-start.13
  332.3 3.3 add_convert_fusion
  335.6 3.9 collective-permute-start.17
  341.5 51.7 %all-reduce.1 = (f32[]{:T(128)}, f32[]{:T(128)}) all-reduce(f32[]{:T(128)} %multiply_reduce_fusion.1, f32[]{:T(128)} %multiply_reduce_fusion), channel_id=1, replica_groups=mesh['seq'=8,'ch'=4] {'seq','ch'}, use_global_device_ids=true, to_apply=%region_1.2 | all-reduce | flops 2 | bytes 16 | tf_op jit(solution)/shard_map/psum | solution.py:254
  395.9 3.2 shard_map.129
  400.1 3.3 shard_map.130
  403.4 2.2 pad_maximum_fusion.4
  (164 shorter events, 43.2 us)
Async XLA Ops:
  2.4 5.8 %copy-start.27 = (bf16[256,1024]{1,0:T(8,128)(2,1)}, bf16[256,1024]{1,0:T(8,128)(2,1)S(1)}, u32[]{:S(2)}) copy-start(bf16[256,1024]{1,0:T(8,128)(2,1)S(1)} %get-tuple-element.93) | copy-start | bytes 1572868
  2.4 5.8 %copy-start.29 = (bf16[256,1024]{1,0:T(8,128)(2,1)}, bf16[256,1024]{1,0:T(8,128)(2,1)S(1)}, u32[]{:S(2)}) copy-start(bf16[256,1024]{1,0:T(8,128)(2,1)S(1)} %get-tuple-element.108) | copy-start | bytes 1572868
  2.4 9.3 %copy-start.35 = (bf16[256,2048]{1,0:T(8,128)(2,1)S(1)}, bf16[256,2048]{1,0:T(8,128)(2,1)}, u32[]{:S(2)}) copy-start(bf16[256,2048]{1,0:T(8,128)(2,1)} %param.14) | copy-start | bytes 3145732
  2.4 9.3 %copy-start.44 = (bf16[256,2048]{1,0:T(8,128)(2,1)S(1)}, bf16[256,2048]{1,0:T(8,128)(2,1)}, u32[]{:S(2)}) copy-start(bf16[256,2048]{1,0:T(8,128)(2,1)} %param.11) | copy-start | bytes 3145732
  3.5 57.9 %collective-permute-start.1 = (bf16[256,2048]{1,0:T(8,128)(2,1)}, bf16[256,2048]{1,0:T(8,128)(2,1)S(1)}, u32[]{:S(2)}, u32[]{:S(2)}) collective-permute-start(bf16[256,2048]{1,0:T(8,128)(2,1)} %pad_maximum_fusion), channel_id=1, source_target_pairs={{0,8},{4,12},{8,16},{12,20},{16,24},{20,28},{1,9},{5,13},{9,17},{1... | collective-permute-start | bytes 3145736 | tf_op jit(solution)/shard_map/ppermute | solution.py:20
  8.2 9.5 %copy-start.53 = (s32[2048]{0:T(1024)S(1)}, s32[2048]{0:T(1024)}, u32[]{:S(2)}) copy-start(s32[2048]{0:T(1024)} %param.15) | copy-start | bytes 24580
  8.2 53.2 %collective-permute-start.2 = (bf16[256,2048]{1,0:T(8,128)(2,1)}, bf16[256,2048]{1,0:T(8,128)(2,1)S(1)}, u32[]{:S(2)}, u32[]{:S(2)}) collective-permute-start(bf16[256,2048]{1,0:T(8,128)(2,1)} %pad_maximum_fusion.1), channel_id=1, source_target_pairs={{0,8},{4,12},{8,16},{12,20},{16,24},{20,28},{1,9},{5,13},{9,17},{1... | collective-permute-start | bytes 3145736 | tf_op jit(solution)/shard_map/ppermute | solution.py:20
  12.2 18.3 %copy-start.26 = (bf16[256,2048]{1,0:T(8,128)(2,1)}, bf16[256,2048]{1,0:T(8,128)(2,1)S(1)}, u32[]{:S(2)}) copy-start(bf16[256,2048]{1,0:T(8,128)(2,1)S(1)} %multiply_convert_fusion) | copy-start | bytes 3145732
  13.1 16.2 %collective-permute-start = (bf16[127,2048]{1,0:T(8,128)(2,1)}, bf16[127,2048]{1,0:T(8,128)(2,1)}, u32[]{:S(2)}, u32[]{:S(2)}) collective-permute-start(bf16[127,2048]{1,0:T(8,128)(2,1)} %slice.124), channel_id=1, source_target_pairs={{4,0},{8,4},{12,8},{16,12},{20,16},{24,20},{28,24},{5,1},{9,5},{13... | collective-permute-start | bytes 1560584 | tf_op jit(solution)/shard_map/ppermute | solution.py:20
  17.8 12.6 %copy-start.47 = (bf16[128,2048]{1,0:T(8,128)(2,1)S(1)}, bf16[128,2048]{1,0:T(8,128)(2,1)}, u32[]{:S(2)}) copy-start(bf16[128,2048]{1,0:T(8,128)(2,1)} %param.13) | copy-start | bytes 1572868
  61.8 26.2 %collective-permute-start.4 = (bf16[256,2048]{1,0:T(8,128)(2,1)S(1)}, bf16[256,2048]{1,0:T(8,128)(2,1)S(1)}, u32[]{:S(2)}, u32[]{:S(2)}) collective-permute-start(bf16[256,2048]{1,0:T(8,128)(2,1)S(1)} %broadcast_select_fusion.2), channel_id=1, source_target_pairs={{0,4},{4,0},{8,12},{12,8},{16,20},{20,16},{24,28},{28,24},{1,5},{5... | collective-permute-start | bytes 3145736 | tf_op jit(solution)/shard_map/ppermute | solution.py:70
  62.9 44.8 %collective-permute-start.3 = (bf16[256,2048]{1,0:T(8,128)(2,1)S(1)}, bf16[256,2048]{1,0:T(8,128)(2,1)S(1)}, u32[]{:S(2)}, u32[]{:S(2)}) collective-permute-start(bf16[256,2048]{1,0:T(8,128)(2,1)S(1)} %broadcast_select_fusion.3), channel_id=1, source_target_pairs={{0,4},{4,0},{8,12},{12,8},{16,20},{20,16},{24,28},{28,24},{1,5},{5... | collective-permute-start | bytes 3145736 | tf_op jit(solution)/shard_map/ppermute | solution.py:70
  64.3 44.4 %collective-permute-start.5 = (bf16[256,2048]{1,0:T(8,128)(2,1)S(1)}, bf16[256,2048]{1,0:T(8,128)(2,1)S(1)}, u32[]{:S(2)}, u32[]{:S(2)}) collective-permute-start(bf16[256,2048]{1,0:T(8,128)(2,1)S(1)} %collective-permute-done.1.refs_6_.refs_11_), channel_id=1, source_target_pairs={{0,8},{4,12},{8,16},{12,20},{16,24},{20,28},{1,9},{5,13},{9,17},{1... | collective-permute-start | bytes 3145736 | tf_op jit(solution)/shard_map/ppermute | solution.py:20
  66.5 45.0 %collective-permute-start.6 = (bf16[256,2048]{1,0:T(8,128)(2,1)S(1)}, bf16[256,2048]{1,0:T(8,128)(2,1)S(1)}, u32[]{:S(2)}, u32[]{:S(2)}) collective-permute-start(bf16[256,2048]{1,0:T(8,128)(2,1)S(1)} %collective-permute-done.2.refs_6_.refs_11_), channel_id=1, source_target_pairs={{0,8},{4,12},{8,16},{12,20},{16,24},{20,28},{1,9},{5,13},{9,17},{1... | collective-permute-start | bytes 3145736 | tf_op jit(solution)/shard_map/ppermute | solution.py:20
  87.9 24.7 %copy-start.20 = (bf16[256,2048]{1,0:T(8,128)(2,1)}, bf16[256,2048]{1,0:T(8,128)(2,1)S(1)}, u32[]{:S(2)}) copy-start(bf16[256,2048]{1,0:T(8,128)(2,1)S(1)} %collective-permute-done.4.refs_7_.refs_12_) | copy-start | bytes 3145732
  113.6 22.2 %collective-permute-start.7 = (bf16[256,2048]{1,0:T(8,128)(2,1)}, bf16[256,2048]{1,0:T(8,128)(2,1)}, u32[]{:S(2)}, u32[]{:S(2)}) collective-permute-start(bf16[256,2048]{1,0:T(8,128)(2,1)} %broadcast_select_fusion.1), channel_id=1, source_target_pairs={{0,4},{4,0},{8,12},{12,8},{16,20},{20,16},{24,28},{28,24},{1,5},{5... | collective-permute-start | bytes 3145736 | tf_op jit(solution)/shard_map/ppermute | solution.py:70
  114.6 21.3 %copy-start.3 = (bf16[256,2048]{1,0:T(8,128)(2,1)S(1)}, bf16[256,2048]{1,0:T(8,128)(2,1)}, u32[]{:S(2)}) copy-start(bf16[256,2048]{1,0:T(8,128)(2,1)} %copy-done.2) | copy-start | bytes 3145732
  114.6 21.3 %copy-start.4 = (bf16[256,2048]{1,0:T(8,128)(2,1)S(1)}, bf16[256,2048]{1,0:T(8,128)(2,1)}, u32[]{:S(2)}) copy-start(bf16[256,2048]{1,0:T(8,128)(2,1)} %refs_8_.2) | copy-start | bytes 3145732
  114.6 21.3 %copy-start.6 = (bf16[256,2048]{1,0:T(8,128)(2,1)S(1)}, bf16[256,2048]{1,0:T(8,128)(2,1)}, u32[]{:S(2)}) copy-start(bf16[256,2048]{1,0:T(8,128)(2,1)} %refs_13_.2) | copy-start | bytes 3145732
  164.2 11.4 %copy-start = (bf16[256,2048]{1,0:T(8,128)(2,1)}, bf16[256,2048]{1,0:T(8,128)(2,1)S(1)}, u32[]{:S(2)}) copy-start(bf16[256,2048]{1,0:T(8,128)(2,1)S(1)} %get-tuple-element.71) | copy-start | bytes 3145732
  164.2 11.4 %copy-start.8 = (bf16[256,2048]{1,0:T(8,128)(2,1)}, bf16[256,2048]{1,0:T(8,128)(2,1)S(1)}, u32[]{:S(2)}) copy-start(bf16[256,2048]{1,0:T(8,128)(2,1)S(1)} %get-tuple-element.70) | copy-start | bytes 3145732
  164.2 11.4 %copy-start.12 = (bf16[256,1024]{1,0:T(8,128)(2,1)}, bf16[256,1024]{1,0:T(8,128)(2,1)S(1)}, u32[]{:S(2)}) copy-start(bf16[256,1024]{1,0:T(8,128)(2,1)S(1)} %get-tuple-element.53) | copy-start | bytes 1572868
  164.2 11.4 %copy-start.14 = (bf16[256,1024]{1,0:T(8,128)(2,1)}, bf16[256,1024]{1,0:T(8,128)(2,1)S(1)}, u32[]{:S(2)}) copy-start(bf16[256,1024]{1,0:T(8,128)(2,1)S(1)} %get-tuple-element.85) | copy-start | bytes 1572868
  164.3 11.1 %collective-permute-start.8 = (bf16[127,1024]{1,0:T(8,128)(2,1)S(1)}, bf16[127,1024]{1,0:T(8,128)(2,1)S(1)}, u32[]{:S(2)}, u32[]{:S(2)}) collective-permute-start(bf16[127,1024]{1,0:T(8,128)(2,1)S(1)} %slice.101), channel_id=1, source_target_pairs={{0,4},{4,8},{8,12},{12,16},{16,20},{20,24},{24,28},{1,5},{5,9},{9,... | collective-permute-start | bytes 780296 | tf_op jit(solution)/shard_map/ppermute | solution.py:20
  168.1 36.8 %collective-permute-start.10 = (bf16[256,2048]{1,0:T(8,128)(2,1)S(1)}, bf16[256,2048]{1,0:T(8,128)(2,1)S(1)}, u32[]{:S(2)}, u32[]{:S(2)}) collective-permute-start(bf16[256,2048]{1,0:T(8,128)(2,1)S(1)} %broadcast_select_fusion), channel_id=1, source_target_pairs={{0,4},{4,0},{8,12},{12,8},{16,20},{20,16},{24,28},{28,24},{1,5},{5... | collective-permute-start | bytes 3145736 | tf_op jit(solution)/shard_map/ppermute | solution.py:70
  168.6 51.8 %collective-permute-start.9 = (bf16[256,2048]{1,0:T(8,128)(2,1)S(1)}, bf16[256,2048]{1,0:T(8,128)(2,1)S(1)}, u32[]{:S(2)}, u32[]{:S(2)}) collective-permute-start(bf16[256,2048]{1,0:T(8,128)(2,1)S(1)} %get-tuple-element.56), channel_id=1, source_target_pairs={{0,4},{4,0},{8,12},{12,8},{16,20},{20,16},{24,28},{28,24},{1,5},{5... | collective-permute-start | bytes 3145736 | tf_op jit(solution)/shard_map/ppermute | solution.py:70
  170.2 155.1 %collective-permute-start.12 = (bf16[256,2048]{1,0:T(8,128)(2,1)}, bf16[256,2048]{1,0:T(8,128)(2,1)}, u32[]{:S(2)}, u32[]{:S(2)}) collective-permute-start(bf16[256,2048]{1,0:T(8,128)(2,1)} %get-tuple-element.73), channel_id=1, source_target_pairs={{0,4},{4,0},{8,12},{12,8},{16,20},{20,16},{24,28},{28,24},{1,5},{5... | collective-permute-start | bytes 3145736 | tf_op jit(solution)/shard_map/ppermute | solution.py:70
  189.5 14.3 %copy-start.36 = (bf16[256,2048]{1,0:T(8,128)(2,1)S(1)}, bf16[256,2048]{1,0:T(8,128)(2,1)}, u32[]{:S(2)}) copy-start(bf16[256,2048]{1,0:T(8,128)(2,1)} %param.14) | copy-start | bytes 3145732
  226.5 74.4 %all-to-all-start = ((f32[8,16,1024]{2,1,0:T(8,128)}), f32[8,16,1024]{2,1,0:T(8,128)}, u32[]{:S(2)}, u32[]{:S(2)}) async-start(f32[8,16,1024]{2,1,0:T(8,128)} %bitcast_dynamic-update-slice_fusion), calls=%async_computation | async-start | bytes 1048576 | tf_op jit(solution)/shard_map/all_to_all | solution.py:242
  238.4 28.5 %copy-start.1 = (bf16[256,2048]{1,0:T(8,128)(2,1)S(1)}, bf16[256,2048]{1,0:T(8,128)(2,1)}, u32[]{:S(2)}) copy-start(bf16[256,2048]{1,0:T(8,128)(2,1)} %copy-done) | copy-start | bytes 3145732
  238.4 28.5 %copy-start.40 = (bf16[256,2048]{1,0:T(8,128)(2,1)S(1)}, bf16[256,2048]{1,0:T(8,128)(2,1)}, u32[]{:S(2)}) copy-start(bf16[256,2048]{1,0:T(8,128)(2,1)} %copy-done.39) | copy-start | bytes 3145732
  263.3 10.6 %copy-start.10 = (bf16[256,2048]{1,0:T(8,128)(2,1)}, bf16[256,2048]{1,0:T(8,128)(2,1)S(1)}, u32[]{:S(2)}) copy-start(bf16[256,2048]{1,0:T(8,128)(2,1)S(1)} %get-tuple-element.76) | copy-start | bytes 3145732
  263.3 9.6 %copy-start.15 = (bf16[256,1024]{1,0:T(8,128)(2,1)S(1)}, bf16[256,1024]{1,0:T(8,128)(2,1)}, u32[]{:S(2)}) copy-start(bf16[256,1024]{1,0:T(8,128)(2,1)} %copy-done.14) | copy-start | bytes 1572868
  263.3 11.6 %collective-permute-start.18 = (bf16[127,1024]{1,0:T(8,128)(2,1)S(1)}, bf16[127,1024]{1,0:T(8,128)(2,1)S(1)}, u32[]{:S(2)}, u32[]{:S(2)}) collective-permute-start(bf16[127,1024]{1,0:T(8,128)(2,1)S(1)} %slice.105), channel_id=1, source_target_pairs={{0,4},{4,8},{8,12},{12,16},{16,20},{20,24},{24,28},{1,5},{5,9},{9,... | collective-permute-start | bytes 780296 | tf_op jit(solution)/shard_map/ppermute | solution.py:20
  266.9 7.0 %copy-start.13 = (bf16[256,1024]{1,0:T(8,128)(2,1)S(1)}, bf16[256,1024]{1,0:T(8,128)(2,1)}, u32[]{:S(2)}) copy-start(bf16[256,1024]{1,0:T(8,128)(2,1)} %copy-done.12) | copy-start | bytes 1572868
  268.3 57.0 %collective-permute-start.11 = (bf16[256,2048]{1,0:T(8,128)(2,1)}, bf16[256,2048]{1,0:T(8,128)(2,1)}, u32[]{:S(2)}, u32[]{:S(2)}) collective-permute-start(bf16[256,2048]{1,0:T(8,128)(2,1)} %add_convert_fusion.3), channel_id=1, source_target_pairs={{8,0},{12,4},{16,8},{20,12},{24,16},{28,20},{9,1},{13,5},{17,9},{2... | collective-permute-start | bytes 3145736 | tf_op jit(solution)/shard_map/ppermute | solution.py:20
  270.8 26.3 %collective-permute-start.14 = (bf16[256,2048]{1,0:T(8,128)(2,1)}, bf16[256,2048]{1,0:T(8,128)(2,1)S(1)}, u32[]{:S(2)}, u32[]{:S(2)}) collective-permute-start(bf16[256,2048]{1,0:T(8,128)(2,1)} %get-tuple-element.78), channel_id=1, source_target_pairs={{0,4},{4,0},{8,12},{12,8},{16,20},{20,16},{24,28},{28,24},{1,5},{5... | collective-permute-start | bytes 3145736 | tf_op jit(solution)/shard_map/ppermute | solution.py:70
  271.4 60.9 %collective-permute-start.16 = (bf16[256,2048]{1,0:T(8,128)(2,1)}, bf16[256,2048]{1,0:T(8,128)(2,1)S(1)}, u32[]{:S(2)}, u32[]{:S(2)}) collective-permute-start(bf16[256,2048]{1,0:T(8,128)(2,1)} %get-tuple-element.79), channel_id=1, source_target_pairs={{0,4},{4,0},{8,12},{12,8},{16,20},{20,16},{24,28},{28,24},{1,5},{5... | collective-permute-start | bytes 3145736 | tf_op jit(solution)/shard_map/ppermute | solution.py:70
  275.1 13.9 %copy-start.46 = (bf16[1,383,1024]{2,1,0:T(8,128)(2,1)}, bf16[1,383,1024]{2,1,0:T(8,128)(2,1)S(1)}, u32[]{:S(2)}) copy-start(bf16[1,383,1024]{2,1,0:T(8,128)(2,1)S(1)} %maximum_bitcast_fusion.2) | copy-start | bytes 2353156
  297.1 10.9 %copy-start.52 = (bf16[128,1,1024]{2,0,1:T(8,128)(2,1)S(1)}, bf16[128,1,1024]{2,0,1:T(8,128)(2,1)}, u32[]{:S(2)}) copy-start(bf16[128,1,1024]{2,0,1:T(8,128)(2,1)} %get-tuple-element.104) | copy-start | bytes 786436
  298.4 33.8 %collective-permute-start.15 = (bf16[256,2048]{1,0:T(8,128)(2,1)}, bf16[256,2048]{1,0:T(8,128)(2,1)}, u32[]{:S(2)}, u32[]{:S(2)}) collective-permute-start(bf16[256,2048]{1,0:T(8,128)(2,1)} %add_convert_fusion.1), channel_id=1, source_target_pairs={{8,0},{12,4},{16,8},{20,12},{24,16},{28,20},{9,1},{13,5},{17,9},{2... | collective-permute-start | bytes 3145736 | tf_op jit(solution)/shard_map/ppermute | solution.py:20
  300.9 30.2 %all-to-all-start.1 = ((f32[8,16,1024]{2,1,0:T(8,128)}), f32[8,16,1024]{2,1,0:T(8,128)}, u32[]{:S(2)}, u32[]{:S(2)}) async-start(f32[8,16,1024]{2,1,0:T(8,128)} %copy.61), calls=%async_computation.1 | async-start | bytes 1048576 | tf_op jit(solution)/shard_map/all_to_all | solution.py:242
  307.9 15.2 %copy-start.37 = (bf16[256,2048]{1,0:T(8,128)(2,1)S(1)}, bf16[256,2048]{1,0:T(8,128)(2,1)}, u32[]{:S(2)}) copy-start(bf16[256,2048]{1,0:T(8,128)(2,1)} %param.14) | copy-start | bytes 3145732
  325.3 7.0 %copy-start.11 = (bf16[256,2048]{1,0:T(8,128)(2,1)S(1)}, bf16[256,2048]{1,0:T(8,128)(2,1)}, u32[]{:S(2)}) copy-start(bf16[256,2048]{1,0:T(8,128)(2,1)} %copy-done.10) | copy-start | bytes 3145732
  328.7 66.6 %collective-permute-start.13 = (bf16[256,2048]{1,0:T(8,128)(2,1)}, bf16[256,2048]{1,0:T(8,128)(2,1)}, u32[]{:S(2)}, u32[]{:S(2)}) collective-permute-start(bf16[256,2048]{1,0:T(8,128)(2,1)} %add_convert_fusion.2), channel_id=1, source_target_pairs={{8,0},{12,4},{16,8},{20,12},{24,16},{28,20},{9,1},{13,5},{17,9},{2... | collective-permute-start | bytes 3145736 | tf_op jit(solution)/shard_map/ppermute | solution.py:20
  332.3 8.2 %copy-start.42 = (bf16[256,1024]{1,0:T(8,128)(2,1)S(1)}, bf16[256,1024]{1,0:T(8,128)(2,1)}, u32[]{:S(2)}) copy-start(bf16[256,1024]{1,0:T(8,128)(2,1)} %fusion.13) | copy-start | bytes 1572868
  332.3 8.1 %copy-start.43 = (bf16[256,1024]{1,0:T(8,128)(2,1)S(1)}, bf16[256,1024]{1,0:T(8,128)(2,1)}, u32[]{:S(2)}) copy-start(bf16[256,1024]{1,0:T(8,128)(2,1)} %fusion.12) | copy-start | bytes 1572868
  335.6 63.5 %collective-permute-start.17 = (bf16[256,2048]{1,0:T(8,128)(2,1)}, bf16[256,2048]{1,0:T(8,128)(2,1)S(1)}, u32[]{:S(2)}, u32[]{:S(2)}) collective-permute-start(bf16[256,2048]{1,0:T(8,128)(2,1)} %add_convert_fusion), channel_id=1, source_target_pairs={{8,0},{12,4},{16,8},{20,12},{24,16},{28,20},{9,1},{13,5},{17,9},{2... | collective-permute-start | bytes 3145736 | tf_op jit(solution)/shard_map/ppermute | solution.py:20
  (27 other events, 52.6 us)

commit v3 on v2

--- a/solution.py
+++ b/solution.py
@@ -128,7 +128,7 @@
     return pl.pallas_call(
         attention_kernel,
         grid=(heads,),
-        in_specs=[pl.BlockSpec((rows, window), lambda h: (0, 0)), whole, whole, whole]
+        in_specs=[pl.BlockSpec((rows, window), lambda h: (0, 0)), whole, whole, first]
         + [first] * SPAN
         + [whole]
         + [second] * SPAN
@@ -196,22 +196,27 @@
 
     conv_grad = (out_grad.astype(f32) * gate_branch.astype(f32)).astype(jnp.bfloat16)
     grad_edge = from_behind(conv_grad[: TAPS - 1], "seq", -1)
-    mixed_grad = anti_conv(jnp.concatenate([conv_grad, grad_edge], 0), mr_filter)
+    grad_ext = jnp.concatenate([conv_grad, grad_edge], 0)
     taps = jnp.arange(TAPS, dtype=jnp.int32)
     mirror = (taps[:, None] + taps[None, :] == TAPS - 1).astype(jnp.bfloat16)
     flipped = jnp.dot(mirror, mr_filter, preferred_element_type=jnp.bfloat16)
 
-    mixed_grad, bias, flipped, *twos = lax.optimization_barrier((mixed_grad, bias, flipped, *twos))
-    ones = [exchange(jnp.where(odd == 1, two, own)) for own, two in zip(owns, twos)]
-    fours = [from_behind(two, "seq", 2) for two in twos]
-    ones, fours = lax.optimization_barrier((ones, fours))
+    bias, flipped, grad_ext = lax.optimization_barrier((bias, flipped, grad_ext))
+    mixed_grads, ones, fours = [], [], []
+    for c, own, two in zip(columns, owns, twos):
+        grad_c = anti_conv(grad_ext[:, c], mr_filter[:, c])
+        grad_c, two, grad_ext = lax.optimization_barrier((grad_c, two, grad_ext))
+        mixed_grads.append(grad_c)
+        ones.append(exchange(jnp.where(odd == 1, two, own)))
+        fours.append(from_behind(two, "seq", 2))
+    ones[0], fours[0] = lax.optimization_barrier((ones[0], fours[0]))
     threes = [exchange(jnp.where(odd == 1, four, two)) for four, two in zip(fours, twos)]
     windows = [list(window) for window in zip(fours, threes, twos, ones)]
 
     size = lax.axis_size("seq")
     tap_rows = TAPS // size
     query_parts, branch_parts, gate_parts, filter_parts, sums = [], [], [], [], []
-    sources = (queries_in, key_branch, mixed_grad, keys_in, values_in, *windows[0])
+    sources = (queries_in, key_branch, mixed_grads[0], keys_in, values_in, *windows[0])
     for chunk in range(CHUNKS):
         cols = columns[chunk]
         mixed, branch_c, query_c, own_t, t4, t3, t2, t1 = attention(
@@ -228,7 +233,15 @@
         gate_c = (out_grad[:, cols].astype(f32) * conv_out).astype(jnp.bfloat16)
         if chunk + 1 < CHUNKS:
             gate_c, filter_part, e3, *rest = lax.optimization_barrier(
-                (gate_c, filter_part, e3, *sources[:5], *windows[chunk + 1])
+                (
+                    gate_c,
+                    filter_part,
+                    e3,
+                    *sources[:2],
+                    mixed_grads[chunk + 1],
+                    *sources[3:5],
+                    *windows[chunk + 1],
+                )
             )
             sources = tuple(rest)
         gate_parts.append(gate_c)
@@ -251,7 +264,8 @@
 
     own_grad = jnp.flip(jnp.concatenate(filter_parts, 1), 0)
     own_taps = lax.dynamic_slice_in_dim(mr_filter, position * tap_rows, tap_rows, 0).astype(f32)
-    norms = lax.psum((jnp.sum(own_taps * own_taps), jnp.sum(own_grad * own_grad)), ("seq", "ch"))
+    norms = jnp.stack([jnp.sum(own_taps * own_taps), jnp.sum(own_grad * own_grad)])
+    norms = lax.psum(lax.psum(norms, "ch"), "seq")
     trust = jnp.sqrt(norms[0]) / jnp.sqrt(norms[1] + 1e-06)
     ends = [last_sum(*terms, odd) for terms in sums]
     return (

time: 411 us -> 352 us (0.86)
  waiting for transfers between devices: 90.3 us -> 49.1 us
  blocking collectives: 51.7 us -> 39.4 us
  local copies, waits for them, and re-layouts: 36.7 us -> 24.9 us
  starting transfers between devices: 50.7 us -> 55.1 us
    ppermute x8, waiting for transfers between devices: 72.6 us -> 28.1 us  [exchange(): return lax.ppermute(array, 'seq', [(i, i ^ 1) for i in range(size)])]
    psum x1 -> x2, blocking collectives: 51.7 us -> 39.4 us  [per_device(): norms = lax.psum(lax.psum(norms, 'ch'), 'seq')]
    unnamed x117 -> x116, local copies, waits for them, and re-layouts: 23.5 us -> 11.8 us
    conv_general_dilated x1 -> x2, matrix products: 28.6 us -> 28.3 us  [anti_conv(): lax.conv_general_dilated(extended[None], kernel, (1,), 'VALID', dimension...]
  transfers between devices with their start and end apart: 21 -> 21, of which waited for: 8 -> 8; matrix products, arithmetic and copies ran while one was open for 32% -> 38% of each run, Pallas kernels for 7% -> 15%
where the time goes in v3:
time: 352 us; the launch traced here: 349 us
  matrix products  87.2 us (25%)
  Pallas kernels  56.1 us (16%)
  starting transfers between devices  55.1 us (16%)
  waiting for transfers between devices  49.1 us (14%)
  blocking collectives  39.4 us (11%)
  other arithmetic  34.4 us (10%)
  local copies, waits for them, and re-layouts  24.9 us (7%)
    pallas_call x2, Pallas kernels, attention(): pl.pallas_call(attention_kernel, grid=(heads,), in_specs=[pl.BlockSpec((r...  49.6 us
    psum x2, blocking collectives, per_device(): norms = lax.psum(lax.psum(norms, 'ch'), 'seq')  39.4 us
    ppermute x11, starting transfers between devices, from_behind(): return lax.ppermute(array, axis, pairs)  33.8 us
    conv_general_dilated x2, matrix products, causal_conv(): lax.conv_general_dilated(extended[None], kernel, (1,), 'VALID', dimension...  30 us
    conv_general_dilated x2, matrix products, anti_conv(): lax.conv_general_dilated(extended[None], kernel, (1,), 'VALID', dimension...  28.3 us
    ppermute x8, waiting for transfers between devices, exchange(): return lax.ppermute(array, 'seq', [(i, i ^ 1) for i in range(size)])  28.1 us
    conv_general_dilated x2, matrix products, filter_corr(): lax.conv_general_dilated(extended[None], kernel, (1,), 'VALID', dimension...  27.8 us
    ppermute x11, waiting for transfers between devices, from_behind(): return lax.ppermute(array, axis, pairs)  21 us
  transfers between devices with their start and end apart: 21, of which 8 were waited for; matrix products, arithmetic and copies ran while one was open for 38% of the time, Pallas kernels for 15%

profile of v3, /device:TPU:14, one launch (start us, length us, event | category | flops | bytes accessed | tf_op | source)
XLA Modules:
  0.0 349.0 jit_solution(14768965089421211964)
XLA Ops:
  0.7 2.1 multiply_convert_fusion
  3.7 2.4 collective-permute-start
  8.4 3.5 collective-permute-start.1
  15.2 5.3 %collective-permute-done = bf16[127,2048]{1,0:T(8,128)(2,1)} collective-permute-done((bf16[127,2048]{1,0:T(8,128)(2,1)}, bf16[127,2048]{1,0:T(8,128)(2,1)}, u32[]{:S(2)}, u32[]{:S(2)}) %collective-permute-start) | collective-permute-done | bytes 520224 | tf_op jit(solution)/shard_map/ppermute | solution.py:20
  21.7 14.2 %fusion.2 = f32[1,256,1024]{2,0,1:T(1,128)S(1)} fusion(bf16[1,383,1024]{2,1,0:T(8,128)(2,1)S(1)} %slice_bitcast_fusion.1, bf16[128,1,1024]{2,0,1:T(8,128)(2,1)S(1)} %copy-done.51), kind=kOutput, calls=%fused_computation.8 | convolution fusion | flops 67108864 | bytes 2095104 | tf_op jit(solution)/shard_map/conv_general_dilated | solution.py:41
  37.0 1.4 broadcast_select_fusion.3
  38.4 3.5 collective-permute-start.3
  43.0 3.1 collective-permute-start.7
  46.1 1.7 multiply_reduce_fusion.1
  47.8 2.1 slice_bitcast_fusion.2
  50.6 12.1 %collective-permute-done.2.refs_7_.refs_12_ = bf16[256,2048]{1,0:T(8,128)(2,1)} collective-permute-done((bf16[256,2048]{1,0:T(8,128)(2,1)}, bf16[256,2048]{1,0:T(8,128)(2,1)}, u32[]{:S(2)}, u32[]{:S(2)}) %collective-permute-start.2) | collective-permute-done | bytes 1048608 | tf_op jit(solution)/shard_map/ppermute | solution.py:70
  62.7 3.6 %collective-permute-done.3.refs_4_.refs_9_ = bf16[256,2048]{1,0:T(8,128)(2,1)S(1)} collective-permute-done((bf16[256,2048]{1,0:T(8,128)(2,1)S(1)}, bf16[256,2048]{1,0:T(8,128)(2,1)S(1)}, u32[]{:S(2)}, u32[]{:S(2)}) %collective-permute-start.3) | collective-permute-done | bytes 1048608 | tf_op jit(solution)/shard_map/ppermute | solution.py:20
  66.5 2.1 collective-permute-start.4
  68.6 14.1 %fusion = f32[1,256,1024]{2,0,1:T(1,128)S(1)} fusion(bf16[1,383,1024]{2,1,0:T(8,128)(2,1)S(1)} %slice_bitcast_fusion, bf16[128,1,1024]{2,0,1:T(8,128)(2,1)S(1)} %get-tuple-element.106), kind=kOutput, calls=%fused_computation.6 | convolution fusion | flops 67108864 | bytes 2095104 | tf_op jit(solution)/shard_map/conv_general_dilated | solution.py:41
  83.0 3.8 %collective-permute-done.7.refs_6_.refs_11_ = bf16[256,2048]{1,0:T(8,128)(2,1)S(1)} collective-permute-done((bf16[256,2048]{1,0:T(8,128)(2,1)}, bf16[256,2048]{1,0:T(8,128)(2,1)S(1)}, u32[]{:S(2)}, u32[]{:S(2)}) %collective-permute-start.7) | collective-permute-done | bytes 1048608 | tf_op jit(solution)/shard_map/ppermute | solution.py:20
  86.8 3.5 collective-permute-start.8
  90.7 1.8 collective-permute-start.10
  92.5 24.8 %shard_map.127 = (bf16[256,1024]{1,0:T(8,128)(2,1)S(1)}, bf16[256,1024]{1,0:T(8,128)(2,1)S(1)}, bf16[256,1024]{1,0:T(8,128)(2,1)S(1)}, f32[256,2048]{1,0:T(8,128...) custom-call(f32[256,1280]{1,0:T(8,128)} %fusion.5.refs_0_, ...), custom_call_target="tpu_custom_call" | custom-call | flops 8053063680 | bytes 15728640 | tf_op jit(solution)/shard_map/pallas_call | solution.py:128
  117.4 2.7 collective-permute-start.5
  120.3 1.4 collective-permute-start.9
  123.8 4.8 %collective-permute-done.5 = bf16[127,1024]{1,0:T(8,128)(2,1)S(1)} collective-permute-done((bf16[127,1024]{1,0:T(8,128)(2,1)S(1)}, bf16[127,1024]{1,0:T(8,128)(2,1)S(1)}, u32[]{:S(2)}, u32[]{:S(2)}) %collective-permute-start.5) | collective-permute-done | bytes 260128 | tf_op jit(solution)/shard_map/ppermute | solution.py:20
  128.8 13.9 %fusion.10 = f32[1,128,1024]{2,0,1:T(1,128)S(1)} fusion(bf16[1,383,1024]{2,1,0:T(8,128)(2,1)S(1)} %maximum_bitcast_fusion, bf16[256,1,1024]{2,0,1:T(8,128)(2,1)S(1)} %get-tuple-element.91), kind=kOutput, calls=%fused_computation.17 | convolution fusion | flops 67108864 | bytes 1832960 | tf_op jit(solution)/shard_map/conv_general_dilated | solution.py:56
  142.7 14.2 %fusion.12 = f32[1,256,1024]{2,0,1:T(1,128)S(1)} fusion(bf16[1,383,1024]{2,1,0:T(8,128)(2,1)S(1)} %maximum_bitcast_fusion, bf16[128,1,1024]{2,0,1:T(8,128)(2,1)S(1)} %get-tuple-element.105), kind=kOutput, calls=%fused_computation.19 | convolution fusion | flops 67108864 | bytes 2095104 | tf_op jit(solution)/shard_map/conv_general_dilated | solution.py:26
  160.0 13.5 %collective-permute-done.6 = bf16[256,2048]{1,0:T(8,128)(2,1)S(1)} collective-permute-done((bf16[256,2048]{1,0:T(8,128)(2,1)S(1)}, bf16[256,2048]{1,0:T(8,128)(2,1)S(1)}, u32[]{:S(2)}, u32[]{:S(2)}) %collective-permute-start.6) | collective-permute-done | bytes 1048608 | tf_op jit(solution)/shard_map/ppermute | solution.py:70
  178.6 4.3 %all-to-all-start = ((f32[8,16,1024]{2,1,0:T(8,128)}), f32[8,16,1024]{2,1,0:T(8,128)}, u32[]{:S(2)}, u32[]{:S(2)}) async-start(f32[8,16,1024]{2,1,0:T(8,128)} %bitcast_dynamic-update-slice_fusion), calls=%async_computation | async-start | bytes 1048576 | tf_op jit(solution)/shard_map/all_to_all | solution.py:255
  182.9 3.1 add_convert_fusion.3
  186.0 2.6 collective-permute-start.11
  191.0 24.8 %shard_map.128 = (bf16[256,1024]{1,0:T(8,128)(2,1)S(1)}, bf16[256,1024]{1,0:T(8,128)(2,1)S(1)}, bf16[256,1024]{1,0:T(8,128)(2,1)S(1)}, f32[256,2048]{1,0:T(8,128...) custom-call(f32[256,1280]{1,0:T(8,128)} %fusion.5.refs_0_, ...), custom_call_target="tpu_custom_call" | custom-call | flops 8053063680 | bytes 15728640 | tf_op jit(solution)/shard_map/pallas_call | solution.py:128
  215.9 3.5 %collective-permute-start.18 = (bf16[127,1024]{1,0:T(8,128)(2,1)S(1)}, bf16[127,1024]{1,0:T(8,128)(2,1)S(1)}, u32[]{:S(2)}, u32[]{:S(2)}) collective-permute-start(bf16[127,1024]{1,0:T(8,128)(2,1)S(1)} %slice.127), channel_id=1, source_target_pairs={{0,4},{4,8},{8,12},{12,16},{16,20},{20,24},{24,28},{1,5},{5,9},{9,... | collective-permute-start | bytes 780296 | tf_op jit(solution)/shard_map/ppermute | solution.py:20
  220.0 1.5 collective-permute-start.16
  223.6 3.5 %collective-permute-done.18 = bf16[127,1024]{1,0:T(8,128)(2,1)S(1)} collective-permute-done((bf16[127,1024]{1,0:T(8,128)(2,1)S(1)}, bf16[127,1024]{1,0:T(8,128)(2,1)S(1)}, u32[]{:S(2)}, u32[]{:S(2)}) %collective-permute-start.18) | collective-permute-done | bytes 260128 | tf_op jit(solution)/shard_map/ppermute | solution.py:20
  228.2 13.9 %fusion.6 = f32[1,128,1024]{2,0,1:T(1,128)S(1)} fusion(bf16[1,383,1024]{2,1,0:T(8,128)(2,1)S(1)} %maximum_bitcast_fusion.1, bf16[256,1,1024]{2,0,1:T(8,128)(2,1)S(1)} %copy-done.46), kind=kOutput, calls=%fused_computation.13 | convolution fusion | flops 67108864 | bytes 1832960 | tf_op jit(solution)/shard_map/conv_general_dilated | solution.py:56
  242.8 2.2 concatenate.54
  245.0 2.1 copy.80
  247.1 2.5 collective-permute-done.14
  251.0 1.9 collective-permute-start.15
  252.9 7.6 %all-to-all-start.1 = ((f32[8,16,1024]{2,1,0:T(8,128)}), f32[8,16,1024]{2,1,0:T(8,128)}, u32[]{:S(2)}, u32[]{:S(2)}) async-start(f32[8,16,1024]{2,1,0:T(8,128)} %copy.80), calls=%async_computation.1 | async-start | bytes 1048576 | tf_op jit(solution)/shard_map/all_to_all | solution.py:255
  260.5 15.8 %fusion.8 = f32[1,256,1024]{2,0,1:T(1,128)} fusion(bf16[1,383,1024]{2,1,0:T(8,128)(2,1)} %copy-done.45, bf16[128,1,1024]{2,0,1:T(8,128)(2,1)S(1)} %copy-done.50), kind=kOutput, calls=%fused_computation.15 | convolution fusion | flops 67108864 | bytes 2095104 | tf_op jit(solution)/shard_map/conv_general_dilated | solution.py:26
  277.5 3.4 add_convert_fusion.2
  280.9 2.5 collective-permute-start.13
  285.3 1.4 pad_maximum_fusion.9
  286.8 3.3 add_convert_fusion
  290.1 4.6 %collective-permute-start.17 = (bf16[256,2048]{1,0:T(8,128)(2,1)}, bf16[256,2048]{1,0:T(8,128)(2,1)}, u32[]{:S(2)}, u32[]{:S(2)}) collective-permute-start(bf16[256,2048]{1,0:T(8,128)(2,1)} %add_convert_fusion), channel_id=1, source_target_pairs={{8,0},{12,4},{16,8},{20,12},{24,16},{28,20},{9,1},{13,5},{17,9},{2... | collective-permute-start | bytes 3145736 | tf_op jit(solution)/shard_map/ppermute | solution.py:20
  295.1 6.0 %psum.14 = f32[2]{0:T(128)S(1)} all-reduce(f32[2]{0:T(128)S(1)} %pad_maximum_fusion.9), channel_id=1, replica_groups=mesh['seq'=8,'ch'=4] {'ch'}, use_global_device_ids=true, to_apply=%region_4.5 | all-reduce | flops 2 | bytes 16 | tf_op jit(solution)/shard_map/psum | solution.py:268
  302.1 33.5 %psum.15 = f32[2]{0:T(128)S(1)} all-reduce(f32[2]{0:T(128)S(1)} %psum.14), channel_id=1, replica_groups=mesh['seq'=8,'ch'=4] {'seq'}, use_global_device_ids=true, to_apply=%region_5.6 | all-reduce | flops 2 | bytes 16 | tf_op jit(solution)/shard_map/psum | solution.py:268
  339.2 3.2 shard_map.129
  342.5 3.3 shard_map.130
  345.8 2.2 pad_maximum_fusion.4
  (170 shorter events, 38.2 us)
Async XLA Ops:
  2.7 17.7 %copy-start.27 = (bf16[256,2048]{1,0:T(8,128)(2,1)}, bf16[256,2048]{1,0:T(8,128)(2,1)S(1)}, u32[]{:S(2)}) copy-start(bf16[256,2048]{1,0:T(8,128)(2,1)S(1)} %multiply_convert_fusion) | copy-start | bytes 3145732
  3.7 16.8 %collective-permute-start = (bf16[127,2048]{1,0:T(8,128)(2,1)}, bf16[127,2048]{1,0:T(8,128)(2,1)}, u32[]{:S(2)}, u32[]{:S(2)}) collective-permute-start(bf16[127,2048]{1,0:T(8,128)(2,1)} %slice.148), channel_id=1, source_target_pairs={{4,0},{8,4},{12,8},{16,12},{20,16},{24,20},{28,24},{5,1},{9,5},{13... | collective-permute-start | bytes 1560584 | tf_op jit(solution)/shard_map/ppermute | solution.py:20
  8.4 28.7 %collective-permute-start.1 = (bf16[256,2048]{1,0:T(8,128)(2,1)}, bf16[256,2048]{1,0:T(8,128)(2,1)S(1)}, u32[]{:S(2)}, u32[]{:S(2)}) collective-permute-start(bf16[256,2048]{1,0:T(8,128)(2,1)} %pad_maximum_fusion.1), channel_id=1, source_target_pairs={{0,8},{4,12},{8,16},{12,20},{16,24},{20,28},{1,9},{5,13},{9,17},{1... | collective-permute-start | bytes 3145736 | tf_op jit(solution)/shard_map/ppermute | solution.py:20
  21.6 14.3 %copy-start.28 = (bf16[383,2048]{1,0:T(8,128)(2,1)}, bf16[383,2048]{1,0:T(8,128)(2,1)S(1)}, u32[]{:S(2)}) copy-start(bf16[383,2048]{1,0:T(8,128)(2,1)S(1)} %pad_maximum_fusion) | copy-start | bytes 4706308
  38.4 24.3 %collective-permute-start.2 = (bf16[256,2048]{1,0:T(8,128)(2,1)}, bf16[256,2048]{1,0:T(8,128)(2,1)}, u32[]{:S(2)}, u32[]{:S(2)}) collective-permute-start(bf16[256,2048]{1,0:T(8,128)(2,1)} %broadcast_select_fusion.3), channel_id=1, source_target_pairs={{0,4},{4,0},{8,12},{12,8},{16,20},{20,16},{24,28},{28,24},{1,5},{5... | collective-permute-start | bytes 3145736 | tf_op jit(solution)/shard_map/ppermute | solution.py:70
  38.4 28.0 %collective-permute-start.3 = (bf16[256,2048]{1,0:T(8,128)(2,1)S(1)}, bf16[256,2048]{1,0:T(8,128)(2,1)S(1)}, u32[]{:S(2)}, u32[]{:S(2)}) collective-permute-start(bf16[256,2048]{1,0:T(8,128)(2,1)S(1)} %collective-permute-done.1.refs_6_.refs_11_), channel_id=1, source_target_pairs={{0,8},{4,12},{8,16},{12,20},{16,24},{20,28},{1,9},{5,13},{9,17},{1... | collective-permute-start | bytes 3145736 | tf_op jit(solution)/shard_map/ppermute | solution.py:20
  43.0 43.8 %collective-permute-start.7 = (bf16[256,2048]{1,0:T(8,128)(2,1)}, bf16[256,2048]{1,0:T(8,128)(2,1)S(1)}, u32[]{:S(2)}, u32[]{:S(2)}) collective-permute-start(bf16[256,2048]{1,0:T(8,128)(2,1)} %pad_maximum_fusion.2), channel_id=1, source_target_pairs={{0,8},{4,12},{8,16},{12,20},{16,24},{20,28},{1,9},{5,13},{9,17},{1... | collective-permute-start | bytes 3145736 | tf_op jit(solution)/shard_map/ppermute | solution.py:20
  66.5 26.0 %collective-permute-start.4 = (bf16[256,2048]{1,0:T(8,128)(2,1)S(1)}, bf16[256,2048]{1,0:T(8,128)(2,1)S(1)}, u32[]{:S(2)}, u32[]{:S(2)}) collective-permute-start(bf16[256,2048]{1,0:T(8,128)(2,1)S(1)} %broadcast_select_fusion.2), channel_id=1, source_target_pairs={{0,4},{4,0},{8,12},{12,8},{16,20},{20,16},{24,28},{28,24},{1,5},{5... | collective-permute-start | bytes 3145736 | tf_op jit(solution)/shard_map/ppermute | solution.py:70
  68.6 21.7 %copy-start.31 = (bf16[256,1024]{1,0:T(8,128)(2,1)S(1)}, bf16[256,1024]{1,0:T(8,128)(2,1)}, u32[]{:S(2)}) copy-start(bf16[256,1024]{1,0:T(8,128)(2,1)} %get-tuple-element.92) | copy-start | bytes 1572868
  68.6 21.7 %copy-start.33 = (bf16[256,1024]{1,0:T(8,128)(2,1)S(1)}, bf16[256,1024]{1,0:T(8,128)(2,1)}, u32[]{:S(2)}) copy-start(bf16[256,1024]{1,0:T(8,128)(2,1)} %get-tuple-element.113) | copy-start | bytes 1572868
  82.7 9.7 %copy-start.19 = (bf16[256,2048]{1,0:T(8,128)(2,1)S(1)}, bf16[256,2048]{1,0:T(8,128)(2,1)}, u32[]{:S(2)}) copy-start(bf16[256,2048]{1,0:T(8,128)(2,1)} %refs_1_.2) | copy-start | bytes 3145732
  82.8 9.7 %copy-start.21 = (bf16[256,2048]{1,0:T(8,128)(2,1)S(1)}, bf16[256,2048]{1,0:T(8,128)(2,1)}, u32[]{:S(2)}) copy-start(bf16[256,2048]{1,0:T(8,128)(2,1)} %refs_2_.2) | copy-start | bytes 3145732
  83.0 9.5 %copy-start.2 = (f32[1,256,1024]{2,1,0:T(8,128)S(1)}, f32[1,256,1024]{2,1,0:T(8,128)}, u32[]{:S(2)}) copy-start(f32[1,256,1024]{2,1,0:T(8,128)} %copy.116) | copy-start | bytes 3145732
  83.0 9.5 %copy-start.5 = (bf16[256,2048]{1,0:T(8,128)(2,1)S(1)}, bf16[256,2048]{1,0:T(8,128)(2,1)}, u32[]{:S(2)}) copy-start(bf16[256,2048]{1,0:T(8,128)(2,1)} %copy-done.4) | copy-start | bytes 3145732
  83.0 9.5 %copy-start.9 = (bf16[256,2048]{1,0:T(8,128)(2,1)S(1)}, bf16[256,2048]{1,0:T(8,128)(2,1)}, u32[]{:S(2)}) copy-start(bf16[256,2048]{1,0:T(8,128)(2,1)} %refs_8_.2) | copy-start | bytes 3145732
  86.8 33.4 %collective-permute-start.8 = (bf16[256,2048]{1,0:T(8,128)(2,1)S(1)}, bf16[256,2048]{1,0:T(8,128)(2,1)S(1)}, u32[]{:S(2)}, u32[]{:S(2)}) collective-permute-start(bf16[256,2048]{1,0:T(8,128)(2,1)S(1)} %collective-permute-done.7.refs_6_.refs_11_), channel_id=1, source_target_pairs={{0,8},{4,12},{8,16},{12,20},{16,24},{20,28},{1,9},{5,13},{9,17},{1... | collective-permute-start | bytes 3145736 | tf_op jit(solution)/shard_map/ppermute | solution.py:20
  90.7 67.4 %collective-permute-start.10 = (bf16[256,2048]{1,0:T(8,128)(2,1)S(1)}, bf16[256,2048]{1,0:T(8,128)(2,1)S(1)}, u32[]{:S(2)}, u32[]{:S(2)}) collective-permute-start(bf16[256,2048]{1,0:T(8,128)(2,1)S(1)} %broadcast_select_fusion), channel_id=1, source_target_pairs={{0,4},{4,0},{8,12},{12,8},{16,20},{20,16},{24,28},{28,24},{1,5},{5... | collective-permute-start | bytes 3145736 | tf_op jit(solution)/shard_map/ppermute | solution.py:70
  117.3 11.4 %copy-start.3 = (bf16[256,2048]{1,0:T(8,128)(2,1)}, bf16[256,2048]{1,0:T(8,128)(2,1)S(1)}, u32[]{:S(2)}) copy-start(bf16[256,2048]{1,0:T(8,128)(2,1)S(1)} %get-tuple-element.73) | copy-start | bytes 3145732
  117.3 11.4 %copy-start.11 = (bf16[256,2048]{1,0:T(8,128)(2,1)}, bf16[256,2048]{1,0:T(8,128)(2,1)S(1)}, u32[]{:S(2)}) copy-start(bf16[256,2048]{1,0:T(8,128)(2,1)S(1)} %get-tuple-element.72) | copy-start | bytes 3145732
  117.3 11.4 %copy-start.15 = (bf16[256,1024]{1,0:T(8,128)(2,1)}, bf16[256,1024]{1,0:T(8,128)(2,1)S(1)}, u32[]{:S(2)}) copy-start(bf16[256,1024]{1,0:T(8,128)(2,1)S(1)} %get-tuple-element.87) | copy-start | bytes 1572868
  117.4 11.4 %copy-start.17 = (bf16[256,1024]{1,0:T(8,128)(2,1)}, bf16[256,1024]{1,0:T(8,128)(2,1)S(1)}, u32[]{:S(2)}) copy-start(bf16[256,1024]{1,0:T(8,128)(2,1)S(1)} %get-tuple-element.54) | copy-start | bytes 1572868
  117.4 11.1 %collective-permute-start.5 = (bf16[127,1024]{1,0:T(8,128)(2,1)S(1)}, bf16[127,1024]{1,0:T(8,128)(2,1)S(1)}, u32[]{:S(2)}, u32[]{:S(2)}) collective-permute-start(bf16[127,1024]{1,0:T(8,128)(2,1)S(1)} %slice.119), channel_id=1, source_target_pairs={{0,4},{4,8},{8,12},{12,16},{16,20},{20,24},{24,28},{1,5},{5,9},{9,... | collective-permute-start | bytes 780296 | tf_op jit(solution)/shard_map/ppermute | solution.py:20
  120.2 8.6 %copy-start = (bf16[256,2048]{1,0:T(8,128)(2,1)}, bf16[256,2048]{1,0:T(8,128)(2,1)S(1)}, u32[]{:S(2)}) copy-start(bf16[256,2048]{1,0:T(8,128)(2,1)S(1)} %collective-permute-done.8.refs_4_.refs_9_) | copy-start | bytes 3145732
  120.3 38.7 %collective-permute-start.9 = (bf16[256,2048]{1,0:T(8,128)(2,1)S(1)}, bf16[256,2048]{1,0:T(8,128)(2,1)S(1)}, u32[]{:S(2)}, u32[]{:S(2)}) collective-permute-start(bf16[256,2048]{1,0:T(8,128)(2,1)S(1)} %broadcast_select_fusion.1), channel_id=1, source_target_pairs={{0,4},{4,0},{8,12},{12,8},{16,20},{20,16},{24,28},{28,24},{1,5},{5... | collective-permute-start | bytes 3145736 | tf_op jit(solution)/shard_map/ppermute | solution.py:70
  121.8 51.7 %collective-permute-start.6 = (bf16[256,2048]{1,0:T(8,128)(2,1)S(1)}, bf16[256,2048]{1,0:T(8,128)(2,1)S(1)}, u32[]{:S(2)}, u32[]{:S(2)}) collective-permute-start(bf16[256,2048]{1,0:T(8,128)(2,1)S(1)} %get-tuple-element.57), channel_id=1, source_target_pairs={{0,4},{4,0},{8,12},{12,8},{16,20},{20,16},{24,28},{28,24},{1,5},{5... | collective-permute-start | bytes 3145736 | tf_op jit(solution)/shard_map/ppermute | solution.py:70
  122.4 155.0 %collective-permute-start.12 = (bf16[256,2048]{1,0:T(8,128)(2,1)}, bf16[256,2048]{1,0:T(8,128)(2,1)}, u32[]{:S(2)}, u32[]{:S(2)}) collective-permute-start(bf16[256,2048]{1,0:T(8,128)(2,1)} %get-tuple-element.75), channel_id=1, source_target_pairs={{0,4},{4,0},{8,12},{12,8},{16,20},{20,16},{24,28},{28,24},{1,5},{5... | collective-permute-start | bytes 3145736 | tf_op jit(solution)/shard_map/ppermute | solution.py:70
  142.7 14.3 %copy-start.34 = (bf16[256,2048]{1,0:T(8,128)(2,1)S(1)}, bf16[256,2048]{1,0:T(8,128)(2,1)}, u32[]{:S(2)}) copy-start(bf16[256,2048]{1,0:T(8,128)(2,1)} %param.14) | copy-start | bytes 3145732
  178.5 10.0 %copy-start.1 = (bf16[256,2048]{1,0:T(8,128)(2,1)S(1)}, bf16[256,2048]{1,0:T(8,128)(2,1)}, u32[]{:S(2)}) copy-start(bf16[256,2048]{1,0:T(8,128)(2,1)} %copy-done) | copy-start | bytes 3145732
  178.6 74.4 %all-to-all-start = ((f32[8,16,1024]{2,1,0:T(8,128)}), f32[8,16,1024]{2,1,0:T(8,128)}, u32[]{:S(2)}, u32[]{:S(2)}) async-start(f32[8,16,1024]{2,1,0:T(8,128)} %bitcast_dynamic-update-slice_fusion), calls=%async_computation | async-start | bytes 1048576 | tf_op jit(solution)/shard_map/all_to_all | solution.py:255
  186.0 35.5 %copy-start.18 = (bf16[256,1024]{1,0:T(8,128)(2,1)S(1)}, bf16[256,1024]{1,0:T(8,128)(2,1)}, u32[]{:S(2)}) copy-start(bf16[256,1024]{1,0:T(8,128)(2,1)} %copy-done.17) | copy-start | bytes 1572868
  186.0 91.5 %collective-permute-start.11 = (bf16[256,2048]{1,0:T(8,128)(2,1)}, bf16[256,2048]{1,0:T(8,128)(2,1)}, u32[]{:S(2)}, u32[]{:S(2)}) collective-permute-start(bf16[256,2048]{1,0:T(8,128)(2,1)} %add_convert_fusion.3), channel_id=1, source_target_pairs={{8,0},{12,4},{16,8},{20,12},{24,16},{28,20},{9,1},{13,5},{17,9},{2... | collective-permute-start | bytes 3145736 | tf_op jit(solution)/shard_map/ppermute | solution.py:20
  215.8 7.8 %copy-start.6 = (bf16[256,2048]{1,0:T(8,128)(2,1)}, bf16[256,2048]{1,0:T(8,128)(2,1)S(1)}, u32[]{:S(2)}) copy-start(bf16[256,2048]{1,0:T(8,128)(2,1)S(1)} %get-tuple-element.79) | copy-start | bytes 3145732
  215.8 7.8 %copy-start.13 = (bf16[256,2048]{1,0:T(8,128)(2,1)}, bf16[256,2048]{1,0:T(8,128)(2,1)S(1)}, u32[]{:S(2)}) copy-start(bf16[256,2048]{1,0:T(8,128)(2,1)S(1)} %get-tuple-element.78) | copy-start | bytes 3145732
  215.8 6.7 %copy-start.16 = (bf16[256,1024]{1,0:T(8,128)(2,1)S(1)}, bf16[256,1024]{1,0:T(8,128)(2,1)}, u32[]{:S(2)}) copy-start(bf16[256,1024]{1,0:T(8,128)(2,1)} %copy-done.15) | copy-start | bytes 1572868
  215.9 11.3 %collective-permute-start.18 = (bf16[127,1024]{1,0:T(8,128)(2,1)S(1)}, bf16[127,1024]{1,0:T(8,128)(2,1)S(1)}, u32[]{:S(2)}, u32[]{:S(2)}) collective-permute-start(bf16[127,1024]{1,0:T(8,128)(2,1)S(1)} %slice.127), channel_id=1, source_target_pairs={{0,4},{4,8},{8,12},{12,16},{16,20},{20,24},{24,28},{1,5},{5,9},{9,... | collective-permute-start | bytes 780296 | tf_op jit(solution)/shard_map/ppermute | solution.py:20
  219.4 30.2 %collective-permute-start.14 = (bf16[256,2048]{1,0:T(8,128)(2,1)}, bf16[256,2048]{1,0:T(8,128)(2,1)S(1)}, u32[]{:S(2)}, u32[]{:S(2)}) collective-permute-start(bf16[256,2048]{1,0:T(8,128)(2,1)} %get-tuple-element.80), channel_id=1, source_target_pairs={{0,4},{4,0},{8,12},{12,8},{16,20},{20,16},{24,28},{28,24},{1,5},{5... | collective-permute-start | bytes 3145736 | tf_op jit(solution)/shard_map/ppermute | solution.py:70
  220.0 66.7 %collective-permute-start.16 = (bf16[256,2048]{1,0:T(8,128)(2,1)}, bf16[256,2048]{1,0:T(8,128)(2,1)S(1)}, u32[]{:S(2)}, u32[]{:S(2)}) collective-permute-start(bf16[256,2048]{1,0:T(8,128)(2,1)} %get-tuple-element.81), channel_id=1, source_target_pairs={{0,4},{4,0},{8,12},{12,8},{16,20},{20,16},{24,28},{28,24},{1,5},{5... | collective-permute-start | bytes 3145736 | tf_op jit(solution)/shard_map/ppermute | solution.py:70
  242.1 7.5 %copy-start.7 = (bf16[256,2048]{1,0:T(8,128)(2,1)S(1)}, bf16[256,2048]{1,0:T(8,128)(2,1)}, u32[]{:S(2)}) copy-start(bf16[256,2048]{1,0:T(8,128)(2,1)} %copy-done.6) | copy-start | bytes 3145732
  249.6 10.9 %copy-start.50 = (bf16[128,1,1024]{2,0,1:T(8,128)(2,1)S(1)}, bf16[128,1,1024]{2,0,1:T(8,128)(2,1)}, u32[]{:S(2)}) copy-start(bf16[128,1,1024]{2,0,1:T(8,128)(2,1)} %get-tuple-element.104) | copy-start | bytes 786436
  251.0 35.7 %collective-permute-start.15 = (bf16[256,2048]{1,0:T(8,128)(2,1)}, bf16[256,2048]{1,0:T(8,128)(2,1)}, u32[]{:S(2)}, u32[]{:S(2)}) collective-permute-start(bf16[256,2048]{1,0:T(8,128)(2,1)} %add_convert_fusion.1), channel_id=1, source_target_pairs={{8,0},{12,4},{16,8},{20,12},{24,16},{28,20},{9,1},{13,5},{17,9},{2... | collective-permute-start | bytes 3145736 | tf_op jit(solution)/shard_map/ppermute | solution.py:20
  252.9 30.4 %all-to-all-start.1 = ((f32[8,16,1024]{2,1,0:T(8,128)}), f32[8,16,1024]{2,1,0:T(8,128)}, u32[]{:S(2)}, u32[]{:S(2)}) async-start(f32[8,16,1024]{2,1,0:T(8,128)} %copy.80), calls=%async_computation.1 | async-start | bytes 1048576 | tf_op jit(solution)/shard_map/all_to_all | solution.py:255
  260.5 16.9 %copy-start.12 = (bf16[256,2048]{1,0:T(8,128)(2,1)S(1)}, bf16[256,2048]{1,0:T(8,128)(2,1)}, u32[]{:S(2)}) copy-start(bf16[256,2048]{1,0:T(8,128)(2,1)} %copy-done.11) | copy-start | bytes 3145732
  277.4 9.3 %copy-start.14 = (bf16[256,2048]{1,0:T(8,128)(2,1)S(1)}, bf16[256,2048]{1,0:T(8,128)(2,1)}, u32[]{:S(2)}) copy-start(bf16[256,2048]{1,0:T(8,128)(2,1)} %copy-done.13) | copy-start | bytes 3145732
  280.9 57.3 %collective-permute-start.13 = (bf16[256,2048]{1,0:T(8,128)(2,1)}, bf16[256,2048]{1,0:T(8,128)(2,1)S(1)}, u32[]{:S(2)}, u32[]{:S(2)}) collective-permute-start(bf16[256,2048]{1,0:T(8,128)(2,1)} %add_convert_fusion.2), channel_id=1, source_target_pairs={{8,0},{12,4},{16,8},{20,12},{24,16},{28,20},{9,1},{13,5},{17,9},{2... | collective-permute-start | bytes 3145736 | tf_op jit(solution)/shard_map/ppermute | solution.py:20
  286.8 8.0 %copy-start.35 = (bf16[256,2048]{1,0:T(8,128)(2,1)S(1)}, bf16[256,2048]{1,0:T(8,128)(2,1)}, u32[]{:S(2)}) copy-start(bf16[256,2048]{1,0:T(8,128)(2,1)} %param.14) | copy-start | bytes 3145732
  286.8 8.0 %copy-start.43 = (f32[1,256,1024]{2,0,1:T(1,128)S(1)}, f32[1,256,1024]{2,0,1:T(1,128)}, u32[]{:S(2)}) copy-start(f32[1,256,1024]{2,0,1:T(1,128)} %fusion.8) | copy-start | bytes 3145732
  290.1 11.0 %copy-start.41 = (bf16[256,1024]{1,0:T(8,128)(2,1)S(1)}, bf16[256,1024]{1,0:T(8,128)(2,1)}, u32[]{:S(2)}) copy-start(bf16[256,1024]{1,0:T(8,128)(2,1)} %fusion.15) | copy-start | bytes 1572868
  290.1 52.4 %collective-permute-start.17 = (bf16[256,2048]{1,0:T(8,128)(2,1)}, bf16[256,2048]{1,0:T(8,128)(2,1)}, u32[]{:S(2)}, u32[]{:S(2)}) collective-permute-start(bf16[256,2048]{1,0:T(8,128)(2,1)} %add_convert_fusion), channel_id=1, source_target_pairs={{8,0},{12,4},{16,8},{20,12},{24,16},{28,20},{9,1},{13,5},{17,9},{2... | collective-permute-start | bytes 3145736 | tf_op jit(solution)/shard_map/ppermute | solution.py:20
  (26 other events, 96.5 us)
